TPU v7x, 256 devices: a whole 4x4x8 slice. The times are simulated.
256 devices in a mesh: leaf: 8 (over y, core), row: 4 (over z_hi), col: 8 (over z_lo, x).
Axes of the slice: x: 4, y: 4, z: 8 (z_hi: 4, z_lo: 2; z = z_hi * 2 + z_lo), core: 2. Of those that a mesh axis runs over, the one named last changes fastest.
Arguments:
- child_blocks: bfloat16 [8, 8192, 8192], P('leaf', None, ('row', 'col')), may hold values from -6 to 6
- child_map: int32 [8, 64], replicated, may hold values from 0 to 63, each once within a row
- merged_map: int32 [4, 60], replicated, may hold values from 0 to 63, as said below
- pivots_one: bfloat16 [4, 2, 256, 256], replicated, may hold values from -0.0234375 to 0.0234375
- pivots_two: bfloat16 [2, 2, 256, 256], replicated, may hold values from -0.015625 to 0.015625
Outputs:
- grand_front: bfloat16 [32, 8, 64, 8192], P(('row', 'col'), 'leaf')
Inputs may be any that keep to these rules, and one draw needn't show every extreme that they name: `child_map`: each row orders all 64 block numbers of a first-level front. `merged_map`: the entries of a row are distinct block numbers of a second-level front.
All inputs are finite; a program needn't handle non-finite values.
Results may differ from a plain program's by a relative error of at most 0.017.
Values may be sent and summed in bfloat16 or wider, within the bound.
No kernel may reach another device: no remote copies, remote signals or barrier semaphores. Data moves between devices by JAX's collectives and lax.ppermute only.
A program may use at most 64 MiB of HBM per device.

v0:
```python
import jax
import jax.numpy as jnp
from jax import lax
from jax.sharding import PartitionSpec as P

BLOCK = 128
PANEL = 256


def partner(x, axis, apart):
    return lax.ppermute(x, axis, [(i, i ^ 1 << apart) for i in range(lax.axis_size(axis))])


def source_blocks(mapping, offset, block_count):
    target = jnp.arange(block_count, dtype=jnp.int32)
    matches = mapping[None, :] == target[:, None]
    present = jnp.any(matches, axis=1)
    anchor = jnp.arange(mapping.shape[0], dtype=jnp.int32) + offset
    source = jnp.sum(jnp.where(matches, anchor[None, :], 0), axis=1)
    return (source, present)


def take_blocks(matrix, source, present, split_axis):
    block_count = source.shape[0]
    if split_axis == 0:
        shaped = matrix.reshape(block_count, BLOCK, matrix.shape[1])
        picked = jnp.take(shaped, source, axis=0)
        picked = jnp.where(present[:, None, None], picked, jnp.zeros_like(picked))
    else:
        shaped = matrix.reshape(matrix.shape[0], block_count, BLOCK)
        picked = jnp.take(shaped, source, axis=1)
        picked = jnp.where(present[None, :, None], picked, jnp.zeros_like(picked))
    return picked.reshape(matrix.shape)


def sibling_swap(values, bit_number):
    return partner(values, "leaf", bit_number)


def regroup_rows(values):
    return lax.all_to_all(values, ("row", "col"), split_axis=0, concat_axis=1, tiled=True)


def merge_halves(values, split_axis, bit_number, my_half):
    staying = lax.dynamic_index_in_dim(values, my_half, split_axis, keepdims=False)
    leaving = lax.dynamic_index_in_dim(values, 1 - my_half, split_axis, keepdims=False)
    arrived = sibling_swap(leaving, bit_number)
    return (staying.astype(jnp.float32) + arrived.astype(jnp.float32)).astype(jnp.bfloat16)


def swap_join(values, split_axis, bit_number, join_axis, leaf_pos):
    my_half = leaf_pos // (1 << bit_number) % 2
    staying = lax.dynamic_index_in_dim(values, my_half, split_axis, keepdims=False)
    leaving = lax.dynamic_index_in_dim(values, 1 - my_half, split_axis, keepdims=False)
    arrived = sibling_swap(leaving, bit_number)
    low_first = jnp.concatenate([staying, arrived], axis=join_axis)
    high_first = jnp.concatenate([arrived, staying], axis=join_axis)
    return jnp.where(my_half == 0, low_first, high_first)


def collect_rows(values, leaf_pos, bit_list):
    for bit_number in bit_list:
        my_half = leaf_pos // (1 << bit_number) % 2
        arrived = sibling_swap(values, bit_number)
        values = jnp.where(my_half == 0, jnp.stack([values, arrived]), jnp.stack([arrived, values]))
    return values


def outer_product(lower_part, panel_rows):
    return lax.dot_general(
        lower_part, panel_rows, (((1,), (1,)), ((), ())), preferred_element_type=jnp.float32
    )


def factor_panels(local_rows, pivots, leaf_pos, bit_list):
    for panel_index in range(2):
        columns = local_rows[:, panel_index * PANEL : (panel_index + 1) * PANEL]
        lower_part = jnp.dot(
            columns, pivots[panel_index], preferred_element_type=jnp.float32
        ).astype(jnp.bfloat16)
        stacked = collect_rows(columns, leaf_pos, bit_list)

        def product(shard_piece, first_row, lower_part=lower_part):
            flattened = shard_piece.reshape(-1, shard_piece.shape[-1])
            return outer_product(lower_part, flattened)

        update = product(lax.all_gather(stacked, ("row", "col"), axis=0, tiled=True), jnp.int32(0))
        local_rows = (local_rows.astype(jnp.float32) - update).astype(jnp.bfloat16)
    return local_rows


def local(child_blocks, child_map, merged_map, pivots_one, pivots_two):
    leaf_pos = lax.axis_index("leaf")
    half_zero = leaf_pos % 2
    half_one = leaf_pos // 2 % 2
    own_rows = child_blocks[0]
    front_size = own_rows.shape[0]
    groups = lax.axis_size("row") * lax.axis_size("col")
    block_count = front_size // BLOCK
    kept_offset = 2 * PANEL // BLOCK
    slab_width = front_size // groups
    quarter = front_size // (4 * groups)
    source, present = source_blocks(child_map[leaf_pos], 0, block_count)
    permuted = take_blocks(own_rows, source, present, 0)
    slab_rows = take_blocks(regroup_rows(permuted), source, present, 1)
    level_one = merge_halves(slab_rows.reshape(2, -1, front_size), 0, 0, half_zero)
    level_one = factor_panels(level_one, pivots_one[leaf_pos // 2], leaf_pos, (0,))
    source, present = source_blocks(merged_map[leaf_pos // 2], kept_offset, block_count)
    wide_rows = take_blocks(level_one, source, present, 1)
    row_count = wide_rows.shape[0]
    split_cols = wide_rows.reshape(row_count, groups, 2, slab_width // 2)
    joined = swap_join(split_cols, 2, 0, 0, leaf_pos)
    columns = lax.all_to_all(
        joined.reshape(2 * row_count, groups * (slab_width // 2)),
        ("row", "col"),
        split_axis=1,
        concat_axis=0,
        tiled=True,
    )
    tall_cols = take_blocks(columns, source, present, 0)
    shaped = tall_cols.reshape(groups, 2, 2, quarter, slab_width // 2)
    joined = swap_join(shaped, 2, 0, 3, leaf_pos)
    rows_two = regroup_rows(joined.reshape(groups * 2 * quarter, slab_width))
    level_two = merge_halves(rows_two.reshape(2, quarter, front_size), 0, 1, half_one)
    level_two = factor_panels(level_two, pivots_two[leaf_pos // 4], leaf_pos, (0, 1))
    return level_two[None, None]


def solution(mesh):
    return jax.shard_map(
        local,
        mesh=mesh,
        in_specs=(P("leaf", None, ("row", "col")), P(), P(), P(), P()),
        out_specs=P(("row", "col"), "leaf", None, None),
        check_vma=False,
    )
```

profile of v0, /device:TPU:1, one launch (start us, length us, event | category | flops | bytes accessed | tf_op | source)
XLA Modules:
  0.0 692.5 jit_solution(6476984067384114901)
XLA Ops:
  8.0 4.9 gather_fusion
  13.0 7.7 %fusion.4 = bf16[32,256,256]{2,1,0:T(8,128)(2,1)} fusion(pred[32,256]{1,0:T(8,128)(4,1)S(1)} %get-tuple-element.19, pred[32,256]{1,0:T(8,128)(4,1)S(1)} %get-tuple-element.20, bf16[32,256,256]{2,1,0:T(8,128)(2,1)} %bitcast.108), kind=kLoop, calls=%fused_computation.12 | loop fusion | flops 4194304 | bytes 8404992 | tf_op jit(solution)/shard_map/jit(_where)/select_n | solution.py:28
  20.7 12.0 %all-to-all-start = ((bf16[32,256,256]{2,1,0:T(8,128)(2,1)}), bf16[32,256,256]{2,1,0:T(8,128)(2,1)}, u32[]{:S(2)}, u32[]{:S(2)}) async-start(bf16[32,256,256]{2,1,0:T(8,128)(2,1)} %fusion.4), calls=%async_computation | async-start | bytes 8388608 | tf_op jit(solution)/shard_map/all_to_all | solution.py:41
  32.9 92.9 %all-to-all-done = bf16[32,256,256]{2,1,0:T(8,128)(2,1)} async-done(((bf16[32,256,256]{2,1,0:T(8,128)(2,1)}), bf16[32,256,256]{2,1,0:T(8,128)(2,1)}, u32[]{:S(2)}, u32[]{:S(2)}) %all-to-all-start) | async-done | bytes 4194336 | tf_op jit(solution)/shard_map/all_to_all | solution.py:41
  125.7 6.5 copy.35
  132.2 6.3 copy.36
  138.6 5.3 gather_fusion.1
  143.8 6.8 copy.37
  150.7 7.3 %gather.27 = bf16[2,128,8192]{2,1,0:T(8,128)(2,1)} reshape(bf16[256,64,128]{2,1,0:T(8,128)(2,1)} %copy.37) | data formatting | bytes 8388608 | tf_op jit(solution)/shard_map/jit(_take)/gather | solution.py:31
  158.0 3.2 select_select_fusion
  165.4 3.9 collective-permute-done
  169.3 2.7 fusion.3
  174.2 77.3 %all-gather.5.cloned.1.call-done = bf16[64,128,256]{2,1,0:T(8,128)(2,1)} async-done(((bf16[2,128,256]{2,1,0:T(8,128)(2,1)}), bf16[64,128,256]{2,1,0:T(8,128)(2,1)}) %all-gather.5.cloned.1.call-update) | async-done | bytes 4194320 | tf_op jit(solution)/shard_map/all_gather | solution.py:87
  251.6 5.1 subtract_convert_fusion
  257.5 3.6 collective-permute-start.2
  264.1 75.0 %all-gather.7.cloned.1.call-done = bf16[64,128,256]{2,1,0:T(8,128)(2,1)} async-done(((bf16[2,128,256]{2,1,0:T(8,128)(2,1)}), bf16[64,128,256]{2,1,0:T(8,128)(2,1)}) %all-gather.7.cloned.1.call-update) | async-done | bytes 4194320 | tf_op jit(solution)/shard_map/all_gather | solution.py:87
  339.0 4.4 fusion.7
  345.4 2.5 gather_fusion.2
  349.7 3.4 collective-permute-start.3
  356.6 54.3 %all_to_all.39 = bf16[256,32,128]{2,0,1:T(8,128)(2,1)} all-to-all(bf16[256,32,128]{2,0,1:T(8,128)(2,1)S(1)} %copy.40), channel_id=1, replica_groups=mesh['leaf'=8,'row'=4,'col'=8] {'row','col'}, dimensions={1} | all-to-all | bytes 4194304 | tf_op jit(solution)/shard_map/all_to_all | solution.py:113
  410.9 2.5 gather_fusion.3
  414.0 2.8 collective-permute-start.4
  421.3 5.3 all-to-all-start.2
  426.7 48.3 %all-to-all-done.2 = bf16[32,128,256]{2,1,0:T(8,128)(2,1)S(1)} async-done(((bf16[32,128,256]{2,1,0:T(8,128)(2,1)}), bf16[32,128,256]{2,1,0:T(8,128)(2,1)S(1)}, u32[]{:S(2)}, u32[]{:S(2)}) %all-to-all-start.2) | async-done | bytes 2097184 | tf_op jit(solution)/shard_map/all_to_all | solution.py:41
  477.5 2.9 reshape.277
  481.7 20.8 %collective-permute-done.5 = bf16[64,8192]{1,0:T(8,128)(2,1)} collective-permute-done((bf16[64,8192]{1,0:T(8,128)(2,1)S(1)}, bf16[64,8192]{1,0:T(8,128)(2,1)}, u32[]{:S(2)}, u32[]{:S(2)}) %collective-permute-start.5) | collective-permute-done | bytes 1048608 | tf_op jit(solution)/shard_map/ppermute | solution.py:11
  504.0 3.7 collective-permute-start.6
  512.8 78.9 %all-gather.9.cloned.1.call-done = bf16[64,2,64,256]{3,2,1,0:T(8,128)(2,1)} async-done(((bf16[2,2,64,256]{3,2,1,0:T(8,128)(2,1)}), bf16[64,2,64,256]{3,2,1,0:T(8,128)(2,1)}) %all-gather.9.cloned.1.call-update) | async-done | bytes 4194320 | tf_op jit(solution)/shard_map/all_gather | solution.py:87
  591.7 3.8 subtract_convert_fusion.1
  595.5 3.4 collective-permute-start.8
  603.7 77.5 %all-gather.11.cloned.1.call-done = bf16[64,2,64,256]{3,2,1,0:T(8,128)(2,1)} async-done(((bf16[2,2,64,256]{3,2,1,0:T(8,128)(2,1)}), bf16[64,2,64,256]{3,2,1,0:T(8,128)(2,1)}) %all-gather.11.cloned.1.call-update) | async-done | bytes 4194320 | tf_op jit(solution)/shard_map/all_gather | solution.py:87
  681.2 4.8 fusion.2
  (75 shorter events, 39.0 us)
Async XLA Ops:
  6.5 245.0 %copy-start = (bf16[4,2,256,256]{3,2,1,0:T(8,128)(2,1)S(1)}, bf16[4,2,256,256]{3,2,1,0:T(8,128)(2,1)}, u32[]{:S(2)}) copy-start(bf16[4,2,256,256]{3,2,1,0:T(8,128)(2,1)} %param.8) | copy-start | bytes 3145732
  20.7 105.0 %all-to-all-start = ((bf16[32,256,256]{2,1,0:T(8,128)(2,1)}), bf16[32,256,256]{2,1,0:T(8,128)(2,1)}, u32[]{:S(2)}, u32[]{:S(2)}) async-start(bf16[32,256,256]{2,1,0:T(8,128)(2,1)} %fusion.4), calls=%async_computation | async-start | bytes 8388608 | tf_op jit(solution)/shard_map/all_to_all | solution.py:41
  32.7 218.8 %all-gather.5.cloned.1.call-start = ((), (), s32[]{:S(2)}) async-start(), calls=%async_computation.3 | async-start | bytes 4325376 | tf_op jit(solution)/shard_map/all_gather | solution.py:87
  161.2 1.9 copy-start.2
  163.2 6.2 collective-permute-start
  172.1 1.4 collective-permute-start.1
  174.1 164.9 %all-gather.7.cloned.1.call-start = ((), (), s32[]{:S(2)}) async-start(), calls=%async_computation.4 | async-start | bytes 4325376 | tf_op jit(solution)/shard_map/all_gather | solution.py:87
  257.5 4.5 collective-permute-start.2
  349.7 5.7 collective-permute-start.3
  414.0 5.0 collective-permute-start.4
  421.3 53.7 %all-to-all-start.2 = ((bf16[32,128,256]{2,1,0:T(8,128)(2,1)}), bf16[32,128,256]{2,1,0:T(8,128)(2,1)S(1)}, u32[]{:S(2)}, u32[]{:S(2)}) async-start(bf16[32,128,256]{2,1,0:T(8,128)(2,1)} %maximum_select_fusion.1), calls=%async_computation.2 | async-start | bytes 4194304 | tf_op jit(solution)/shard_map/all_to_all | solution.py:41
  426.6 165.1 %all-gather.9.cloned.1.call-start = ((), (), s32[]{:S(2)}) async-start(), calls=%async_computation.5 | async-start | bytes 4325376 | tf_op jit(solution)/shard_map/all_gather | solution.py:87
  480.4 22.1 %collective-permute-start.5 = (bf16[64,8192]{1,0:T(8,128)(2,1)S(1)}, bf16[64,8192]{1,0:T(8,128)(2,1)}, u32[]{:S(2)}, u32[]{:S(2)}) collective-permute-start(bf16[64,8192]{1,0:T(8,128)(2,1)S(1)} %dynamic-slice_bitcast_fusion.1), channel_id=1, source_target_pairs={{0,64},{32,96},{64,0},{96,32},{128,192},{160,224},{192,128},{224,1... | collective-permute-start | bytes 3145736 | tf_op jit(solution)/shard_map/ppermute | solution.py:11
  504.0 4.6 collective-permute-start.6
  508.7 3.4 collective-permute-start.7
  512.8 168.4 %all-gather.11.cloned.1.call-start = ((), (), s32[]{:S(2)}) async-start(), calls=%async_computation.6 | async-start | bytes 4325376 | tf_op jit(solution)/shard_map/all_gather | solution.py:87
  595.5 4.3 collective-permute-start.8
  599.8 3.2 collective-permute-start.9
  681.2 4.8 copy-start.1
Sparse Core Ops, SparseCore 0:
  174.3 77.2 all-gather.4
  262.8 76.1 all-gather.6
  512.9 78.7 all-gather.8
  603.8 77.3 all-gather.10
where the time goes:
time: 695 us; the launch traced here: 693 us
  waiting for transfers between devices  487 us (70%)
  local copies, waits for them, and re-layouts  56.2 us (8%)
  blocking collectives  54.3 us (8%)
  starting transfers between devices  41.2 us (6%)
  other arithmetic  22.6 us (3%)
  matrix products  18.1 us (3%)
  between operations  13.5 us (2%)
    all_gather x4, waiting for transfers between devices, factor_panels(): lax.all_gather(stacked, ('row', 'col'), axis=0, tiled=True)  309 us
    all_to_all x2, waiting for transfers between devices, regroup_rows(): lax.all_to_all(values, ('row', 'col'), split_axis=0, concat_axis=1, tiled...  141 us
    all_to_all x1, blocking collectives, local(): lax.all_to_all(joined.reshape(2 * row_count, groups * (slab_width // 2)),...  54.3 us
    ppermute x10, waiting for transfers between devices, partner(): lax.ppermute(x, axis, [(i, i ^ 1 << apart) for i in range(lax.axis_size(a...  36.6 us
    ppermute x10, starting transfers between devices, partner(): lax.ppermute(x, axis, [(i, i ^ 1 << apart) for i in range(lax.axis_size(a...  23.7 us
    gather x4, local copies, waits for them, and re-layouts, take_blocks(): picked = jnp.take(shaped, source, axis=1)  22 us
    dot_general x4, matrix products, outer_product(): lax.dot_general(lower_part, panel_rows, (((1,), (1,)), ((), ())), preferr...  18.1 us
    all_to_all x2, starting transfers between devices, regroup_rows(): lax.all_to_all(values, ('row', 'col'), split_axis=0, concat_axis=1, tiled...  17.3 us
  transfers between devices with their start and end apart: 16, of which 16 were waited for; matrix products, arithmetic and copies ran while one was open for 0% of the time, Pallas kernels for 0%

commit v1 on v0

v1 whole, which is shorter than its diff:
```python
import jax
import jax.numpy as jnp
from jax import lax
from jax.experimental import pallas as pl
from jax.experimental.pallas import tpu as pltpu
from jax.sharding import Mesh, PartitionSpec as P

BLOCK = 128
PANEL = 256
NB = 64
NZ = 8
NX = 4
HALF = NB // 2
BF = jnp.bfloat16
F32 = jnp.float32
VMEM = 48 * 1024 * 1024


def params():
    return pltpu.CompilerParams(vmem_limit_bytes=VMEM)


def shift(v, axis, step, n):
    return lax.ppermute(v, axis, [(i, (i + step) % n) for i in range(n)])


def flip(v, axis):
    return lax.ppermute(v, axis, [(0, 1), (1, 0)])


def ring(v, axis, n):
    out = {0: v}
    up = down = v
    half = v.shape[0] // 2
    for s in range(1, n // 2):
        up = shift(up, axis, 1, n)
        down = shift(down, axis, -1, n)
        out[n - s] = up
        out[s] = down
    a = shift(up[:half], axis, 1, n)
    b = shift(down[half:], axis, -1, n)
    out[n // 2] = jnp.concatenate([a, b], axis=0)
    return jnp.stack([out[j] for j in range(n)])


def onehot_pick(table, index):
    hit = index[:, None] == jnp.arange(table.shape[0], dtype=jnp.int32)[None, :]
    return jnp.sum(jnp.where(hit, table[None, :], 0), axis=1).astype(jnp.int32)


def block_maps(child_row, merged_row):
    target = jnp.arange(NB, dtype=jnp.int32)
    hits = merged_row[None, :] == target[:, None]
    filled = jnp.any(hits, axis=1)
    place = jnp.sum(jnp.where(hits, jnp.arange(merged_row.shape[0], dtype=jnp.int32)[None, :] + 4, 0), axis=1)
    before = target[None, :] < target[:, None]
    rank = jnp.sum(jnp.where(before & ~filled[None, :], 1, 0), axis=1)
    first_index = jnp.where(filled, place, rank).astype(jnp.int32)
    child_hits = child_row[None, :] == first_index[:, None]
    source = jnp.sum(jnp.where(child_hits, target[None, :], 0), axis=1).astype(jnp.int32)
    wanted = jnp.arange(4, dtype=jnp.int32)
    pivot = (~filled)[None, :] & (rank[None, :] == wanted[:, None])
    pivot_places = jnp.sum(jnp.where(pivot, target[None, :], 0), axis=1).astype(jnp.int32)
    return source, filled.astype(jnp.int32), pivot_places


def panel_blocks(rows, source, ok, core):
    def body(src, okr, ce, a, keep, send):
        s = pl.program_id(0)
        e = ce[0]
        for out, r in ((keep, e), (send, 1 - e)):
            part = a[0, pl.ds(pl.multiple_of(r * BLOCK, BLOCK), BLOCK), :]
            out[...] = jnp.where(okr[s * 2 + r] > 0, part, jnp.zeros_like(part))
    one = jax.ShapeDtypeStruct((BLOCK, 8 * BLOCK), BF)
    return pl.pallas_call(
        body,
        out_shape=(one, one),
        grid_spec=pltpu.PrefetchScalarGridSpec(
            num_scalar_prefetch=3,
            grid=(8,),
            in_specs=[pl.BlockSpec((1, 2 * BLOCK, BLOCK), lambda i, s, o, c: (s[i] // 2, 0, s[i] % 2))],
            out_specs=[pl.BlockSpec((BLOCK, BLOCK), lambda i, s, o, c: (0, i))] * 2,
        ),
        compiler_params=params(),
    )(source, ok, core, rows)


def few_blocks(rows, source):
    few = rows.shape[1]

    def body(src, *refs):
        for i in range(6):
            refs[-1][:, i * BLOCK:(i + 1) * BLOCK] = refs[i][0]

    def where_from(i):
        return lambda g, s: (s[i] // 2, 0, s[i] % 2)
    return pl.pallas_call(
        body,
        out_shape=jax.ShapeDtypeStruct((few, 6 * BLOCK), BF),
        grid_spec=pltpu.PrefetchScalarGridSpec(
            num_scalar_prefetch=1,
            grid=(1,),
            in_specs=[pl.BlockSpec((1, few, BLOCK), where_from(i)) for i in range(6)],
            out_specs=pl.BlockSpec((few, 6 * BLOCK), lambda g, s: (0, 0)),
        ),
        compiler_params=params(),
    )(source, *[rows] * 6)


def tile_parts(rows, source, ok):
    def body(src, okr, *refs):
        k, x = pl.program_id(0), pl.program_id(1)
        o = refs[-1]
        for z in range(NZ):
            c = 2 * (z * NX + x) + k
            for r in range(2):
                part = refs[z][0, r * BLOCK:(r + 1) * BLOCK, :]
                o[r, 0, 0, z] = jnp.where(okr[c * 2 + r] > 0, part, jnp.zeros_like(part))

    def where_from(z):
        def index(k, x, s, o):
            b = s[2 * (z * NX + x) + k]
            return (b // 2, 0, b % 2)
        return index
    return pl.pallas_call(
        body,
        out_shape=jax.ShapeDtypeStruct((2, 2, NX, NZ, BLOCK, BLOCK), BF),
        grid_spec=pltpu.PrefetchScalarGridSpec(
            num_scalar_prefetch=2,
            grid=(2, NX),
            in_specs=[pl.BlockSpec((1, 2 * BLOCK, BLOCK), where_from(z)) for z in range(NZ)],
            out_specs=pl.BlockSpec((2, 1, 1, NZ, BLOCK, BLOCK), lambda k, x, s, o: (0, k, x, 0, 0, 0)),
        ),
        compiler_params=params(),
    )(source, ok, *[rows] * NZ)


def mm(a, b):
    return jnp.dot(a, b, preferred_element_type=F32)


def mm_t(a, b):
    return lax.dot_general(a, b, (((1,), (1,)), ((), ())), preferred_element_type=F32)


def factor_rows(mine, other, special, w_one, w_two, yp):
    n = PANEL

    def body(y, a_ref, b_ref, s_ref, w1, w2, c_out, l_out):
        low = y[0] == 0
        a, b = a_ref[...], b_ref[...]
        both = (jnp.where(low, a, b), jnp.where(low, b, a))
        panel = (a[:, 2 * n:].astype(F32) + b[:, 2 * n:].astype(F32)).astype(BF).astype(F32)
        lead = s_ref[2 * n:, 4 * n:].astype(F32)
        for p in range(2):
            piv = s_ref[:n, 2 * p * n:(2 * p + 1) * n]
            t0 = s_ref[n:, 2 * p * n:(2 * p + 1) * n]
            t1 = s_ref[n:, (2 * p + 1) * n:(2 * p + 2) * n].astype(F32)
            tl0 = mm(t0, w1[p, 0]).astype(BF)
            tc1 = (t1 - mm_t(tl0, piv)).astype(BF)
            tl1 = mm(tc1[n:], w1[p, 1]).astype(BF)
            lead = lead - mm_t(tl0[n:], t0[:n]) - mm_t(tl1, tc1[:n])
            c0 = both[p][:, :n]
            l0 = mm(c0, w1[p, 0]).astype(BF)
            c1 = (both[p][:, n:2 * n].astype(F32) - mm_t(l0, piv)).astype(BF)
            l1 = mm(c1, w1[p, 1]).astype(BF)
            panel = panel - mm_t(l0, t0) - mm_t(l1, tc1)
            c_out[:, 2 * p * n:(2 * p + 1) * n] = c0
            c_out[:, (2 * p + 1) * n:(2 * p + 2) * n] = c1
            l_out[:, 2 * p * n:(2 * p + 1) * n] = l0
            l_out[:, (2 * p + 1) * n:(2 * p + 2) * n] = l1
        d0 = panel[:, :n].astype(BF)
        k0 = mm(d0, w2[0]).astype(BF)
        d1 = (panel[:, n:] - mm_t(k0, lead.astype(BF))).astype(BF)
        k1 = mm(d1, w2[1]).astype(BF)
        c_out[:, 4 * n:5 * n] = d0
        c_out[:, 5 * n:] = d1
        l_out[:, 4 * n:5 * n] = k0
        l_out[:, 5 * n:] = k1

    out = jax.ShapeDtypeStruct((BLOCK, 6 * n), BF)
    vm = pl.BlockSpec(memory_space=pltpu.VMEM)
    return pl.pallas_call(
        body,
        out_shape=(out, out),
        in_specs=[pl.BlockSpec(memory_space=pltpu.SMEM)] + [vm] * 5,
        out_specs=(vm, vm),
        compiler_params=params(),
    )(yp, mine, other, special, w_one, w_two)


def tile_update(parts, lower, columns, place):
    depth = lower.shape[-1]
    half = BLOCK // 2

    def body(zs, parts_ref, l_ref, c_ref, o_ref):
        c = c_ref[0]
        for x in range(NX):
            total = None
            for pair in range(2):
                s = (parts_ref[2 * pair, x, 0].astype(F32) + parts_ref[2 * pair + 1, x, 0].astype(F32)).astype(BF).astype(F32)
                total = s if total is None else total + s
            done = (total - mm_t(l_ref[(x + NX - zs[1]) % NX], c)).astype(BF)
            o_ref[x, 0] = done[:half]
            o_ref[NX + x, 0] = done[half:]

    return pl.pallas_call(
        body,
        out_shape=jax.ShapeDtypeStruct((2 * NX, NZ, half, BLOCK), BF),
        grid_spec=pltpu.PrefetchScalarGridSpec(
            num_scalar_prefetch=1,
            grid=(NZ,),
            in_specs=[
                pl.BlockSpec((4, NX, 1, BLOCK, BLOCK), lambda j, s: (0, 0, (s[0] + j) % NZ, 0, 0)),
                pl.BlockSpec((NX, BLOCK, depth), lambda j, s: (0, 0, 0)),
                pl.BlockSpec((1, BLOCK, depth), lambda j, s: (j, 0, 0)),
            ],
            out_specs=pl.BlockSpec((2 * NX, 1, half, BLOCK), lambda j, s: (0, (s[0] + j) % NZ, 0, 0)),
        ),
        compiler_params=params(),
    )(place, parts, lower, columns)


def join_rows(pieces):
    half = BLOCK // 2

    def body(a, o):
        for k in range(2):
            for x in range(NX):
                c = 2 * x + k
                o[:, c * BLOCK:(c + 1) * BLOCK] = a[k * NX + x, 0]
    return pl.pallas_call(
        body,
        out_shape=jax.ShapeDtypeStruct((half, NB * BLOCK), BF),
        grid=(NZ,),
        in_specs=[pl.BlockSpec((2 * NX, 1, half, BLOCK), lambda z: (0, z, 0, 0))],
        out_specs=pl.BlockSpec((half, 2 * NX * BLOCK), lambda z: (0, z)),
        compiler_params=params(),
    )(pieces)


def local(child_blocks, child_map, merged_map, pivots_one, pivots_two):
    q, yp, e = lax.axis_index("q"), lax.axis_index("yp"), lax.axis_index("core")
    z, x = lax.axis_index("z"), lax.axis_index("x")
    child = (q * 2 + yp) * 2 + e
    spot = z * NX + x
    slab = child_blocks[0].reshape(NB, BLOCK, 2 * BLOCK)
    source, filled, pivot_places = block_maps(child_map[child], merged_map[child // 2])

    own_filled = lax.dynamic_slice_in_dim(filled, 2 * spot, 2)
    lead_filled = filled[:4]
    panel_src = onehot_pick(source, jnp.concatenate([pivot_places, jnp.arange(4, dtype=jnp.int32)]))
    col_ok = jnp.concatenate([jnp.ones((4,), jnp.int32), lead_filled])

    row_src = onehot_pick(source, jnp.concatenate([pivot_places[2:], jnp.arange(4, dtype=jnp.int32)]))
    few = 6 * BLOCK // (NZ * NX)
    first = jnp.take(slab, row_src, axis=0).reshape(NZ * NX, few, 2 * BLOCK)
    first = lax.all_to_all(first, ("z", "x"), split_axis=0, concat_axis=0, tiled=True)
    part_of = (spot * few + jnp.arange(few, dtype=jnp.int32)) // BLOCK
    row_ok = onehot_pick(jnp.concatenate([jnp.ones((2,), jnp.int32), lead_filled]), part_of)
    first = few_blocks(first, panel_src)
    first_ok = (row_ok[:, None] * jnp.repeat(col_ok, BLOCK)[None, :6 * BLOCK]) > 0
    first = jnp.where(first_ok, first, jnp.zeros_like(first))
    first = (first.astype(F32) + flip(first, "core").astype(F32)).astype(BF)
    second = flip(first, "yp")
    low = jnp.where(yp == 0, first, second)
    high = jnp.where(yp == 0, second, first)
    lead = (low[:, 2 * PANEL:].astype(F32) + high[:, 2 * PANEL:].astype(F32)).astype(BF)
    special = jnp.concatenate([low[:, :2 * PANEL], high[:, :2 * PANEL], lead], axis=1)
    special = lax.all_gather(special, ("z", "x"), axis=0, tiled=True)

    sent = jnp.take(slab, source, axis=0).reshape(NZ * NX, 2 * BLOCK, 2 * BLOCK)
    rows = lax.all_to_all(sent, ("z", "x"), split_axis=0, concat_axis=0, tiled=True)

    panel_ok = (col_ok[:, None] * own_filled[None, :]).reshape(-1)
    keep, send = panel_blocks(rows, panel_src, panel_ok, e.reshape(1))
    got = flip(send, "core")
    mine = (keep.astype(F32) + got.astype(F32)).astype(BF)
    other = flip(mine, "yp")
    w_one = lax.dynamic_slice_in_dim(pivots_one, 2 * q, 2)
    w_two = lax.dynamic_index_in_dim(pivots_two, q, keepdims=False)
    columns, lower = factor_rows(mine, other, special, w_one, w_two, yp.reshape(1))

    tile_ok = (filled[:, None] * own_filled[None, :]).reshape(-1)
    parts = tile_parts(rows, source, tile_ok)
    parts = lax.all_to_all(parts.reshape(4 * NX, NZ, BLOCK, BLOCK), ("yp", "core", "x"), split_axis=0, concat_axis=0, tiled=True)

    columns = ring(columns, "z", NZ)
    swapped = flip(lower, "core")
    lower = ring(jnp.where(e == yp, lower, swapped), "x", NX)

    done = tile_update(parts.reshape(4, NX, NZ, BLOCK, BLOCK), lower, columns, jnp.stack([z, x]))
    done = lax.all_to_all(done, ("core", "x"), split_axis=0, concat_axis=0, tiled=True)
    return join_rows(done)[None, None]


def solution(mesh):
    fine = Mesh(mesh.devices.reshape(2, 2, 2, NZ, NX), ("q", "yp", "core", "z", "x"))
    leaf, plane = ("q", "yp", "core"), ("z", "x")
    return jax.shard_map(
        local,
        mesh=fine,
        in_specs=(P(leaf, None, plane), P(), P(), P(), P()),
        out_specs=P(plane, leaf, None, None),
        check_vma=False,
    )
```

time: 695 us -> 295 us (0.42)
  waiting for transfers between devices: 487 us -> 160 us
  local copies, waits for them, and re-layouts: 56.2 us -> 17.6 us
  blocking collectives: 54.3 us -> 21 us
  Pallas kernels: 0 us -> 24.5 us
  matrix products: 18.1 us -> 0 us
  other arithmetic: 22.6 us -> 8.88 us
  starting transfers between devices: 41.2 us -> 48.5 us
    all_gather x4 -> x1, waiting for transfers between devices: 309 us -> 0.01 us  [local(): special = lax.all_gather(special, ('z', 'x'), axis=0, tiled=True)]
    all_to_all x2 -> x3, waiting for transfers between devices: 141 us -> 95.7 us  [the longest x1 92.4 us: local(): lax.all_to_all(sent, ('z', 'x'), split_axis=0, concat_axis=0, tiled=True)]
    all_to_all x1, blocking collectives: 54.3 us -> 21 us  [local(): lax.all_to_all(done, ('core', 'x'), split_axis=0, concat_axis=0, tiled=True)]
    ppermute x10 -> x17, waiting for transfers between devices: 36.6 us -> 64.2 us  [the longest x12 59 us: shift(): return lax.ppermute(v, axis, [(i, (i + step) % n) for i in range(n)])]
    pallas_call x0 -> x6, Pallas kernels: none -> 24.5 us  [the longest x1 7.92 us: tile_update(): pl.pallas_call(body, out_shape=jax.ShapeDtypeStruct((2 * NX, NZ, half, BL...]
    gather x6 -> x2, local copies, waits for them, and re-layouts: 29.5 us -> 7.71 us  [the longest x1 4.95 us: local(): sent = jnp.take(slab, source, axis=0).reshape(NZ * NX, 2 * BLOCK, 2 * BLOCK)]
    dot_general x4 -> x0, matrix products: 18.1 us -> none  [outer_product(): lax.dot_general(lower_part, panel_rows, (((1,), (1,)), ((), ())), preferr...]
    select_n x16 -> x9, other arithmetic: 17.9 us -> 6.35 us  [the longest x2 5.28 us: local(): sent = jnp.take(slab, source, axis=0).reshape(NZ * NX, 2 * BLOCK, 2 * BLOCK)]
  transfers between devices with their start and end apart: 16 -> 21, of which waited for: 16 -> 11; matrix products, arithmetic and copies ran while one was open for 0% -> 4% of each run, Pallas kernels for 0% -> 5%
where the time goes in v1:
time: 295 us; the launch traced here: 294 us
  waiting for transfers between devices  160 us (54%)
  starting transfers between devices  48.5 us (16%)
  Pallas kernels  24.5 us (8%)
  blocking collectives  21 us (7%)
  local copies, waits for them, and re-layouts  17.6 us (6%)
  between operations  13.8 us (5%)
  other arithmetic  8.88 us (3%)
    all_to_all x1, waiting for transfers between devices, local(): lax.all_to_all(sent, ('z', 'x'), split_axis=0, concat_axis=0, tiled=True)  92.4 us
    ppermute x12, waiting for transfers between devices, shift(): return lax.ppermute(v, axis, [(i, (i + step) % n) for i in range(n)])  59 us
    all_to_all x1, blocking collectives, local(): lax.all_to_all(done, ('core', 'x'), split_axis=0, concat_axis=0, tiled=True)  21 us
    ppermute x12, starting transfers between devices, shift(): return lax.ppermute(v, axis, [(i, (i + step) % n) for i in range(n)])  15.5 us
    all_to_all x1, starting transfers between devices, local(): lax.all_to_all(first, ('z', 'x'), split_axis=0, concat_axis=0, tiled=True)  11.9 us
    ppermute x5, starting transfers between devices, flip(): return lax.ppermute(v, axis, [(0, 1), (1, 0)])  9.2 us
    pallas_call x1, Pallas kernels, tile_update(): pl.pallas_call(body, out_shape=jax.ShapeDtypeStruct((2 * NX, NZ, half, BL...  7.92 us
    unnamed x19, local copies, waits for them, and re-layouts  7.27 us
  transfers between devices with their start and end apart: 21, of which 11 were waited for; matrix products, arithmetic and copies ran while one was open for 4% of the time, Pallas kernels for 5%

profile of v1, /device:TPU:1, one launch (start us, length us, event | category | flops | bytes accessed | tf_op | source)
XLA Modules:
  0.0 294.2 jit_solution(8175689948850176249)
XLA Ops:
  9.2 2.8 gather_fusion.1
  12.9 11.9 %all-to-all-start.2 = ((bf16[32,24,256]{2,1,0:T(8,128)(2,1)}), bf16[32,24,256]{2,1,0:T(8,128)(2,1)S(1)}, u32[]{:S(2)}, u32[]{:S(2)}) async-start(bf16[32,24,256]{2,1,0:T(8,128)(2,1)} %broadcast_select_fusion), calls=%async_computation.2 | async-start | bytes 786432 | tf_op jit(solution)/shard_map/all_to_all | solution.py:258
  24.9 5.0 %gather_fusion = bf16[64,128,256]{2,1,0:T(8,128)(2,1)} fusion(bf16[64,128,256]{2,1,0:T(8,128)(2,1)} %bitcast.59, s32[1024]{0:T(1024)S(1)} %pad_clamp_fusion.1), kind=kCustom, calls=%fused_computation | custom fusion | bytes 8388864 | tf_op jit(solution)/shard_map/jit(_take)/gather | solution.py:272
  30.0 5.3 %bitcast_select_fusion = bf16[32,256,256]{2,1,0:T(8,128)(2,1)} fusion(pred[32,256]{1,0:T(8,128)(4,1)S(1)} %bitcast.65, bf16[32,256,256]{2,1,0:T(8,128)(2,1)} %bitcast.57), kind=kLoop, calls=%fused_computation.2 | loop fusion | flops 2097152 | bytes 8396800 | tf_op jit(solution)/shard_map/jit(_take)/select_n | solution.py:272
  35.3 3.3 %all-to-all-done.2.refs_0_.refs_1_.refs_2_.refs_3_.refs_4_.refs_5_ = bf16[32,24,256]{2,1,0:T(8,128)(2,1)S(1)} async-done(((bf16[32,24,256]{2,1,0:T(8,128)(2,1)}), bf16[32,24,256]{2,1,0:T(8,128)(2,1)S(1)}, u32[]{:S(2)}, u32[]{:S(2)}) %all-to-all-start.2) | async-done | bytes 393248 | tf_op jit(solution)/shard_map/all_to_all | solution.py:258
  38.6 6.0 %all-to-all-start = ((bf16[32,256,256]{2,1,0:T(8,128)(2,1)}), bf16[32,256,256]{2,1,0:T(8,128)(2,1)}, u32[]{:S(2)}, u32[]{:S(2)}) async-start(bf16[32,256,256]{2,1,0:T(8,128)(2,1)} %bitcast_select_fusion), calls=%async_computation | async-start | bytes 8388608 | tf_op jit(solution)/shard_map/all_to_all | solution.py:273
  45.9 1.6 collective-permute-start.2
  49.8 1.9 collective-permute-done.3
  52.8 92.4 %all-to-all-done.refs_0_.refs_1_.refs_2_.refs_3_.refs_4_.refs_5_.refs_6_.refs_7_.a = bf16[32,256,256]{2,1,0:T(8,128)(2,1)} async-done(((bf16[32,256,256]{2,1,0:T(8,128)(2,1)}), bf16[32,256,256]{2,1,0:T(8,128)(2,1)}, u32[]{:S(2)}, u32[]{:S(2)}) %all-to-all-start) | async-done | bytes 4194336 | tf_op jit(solution)/shard_map/all_to_all | solution.py:273
  145.1 4.3 %shard_map.56 = (bf16[128,1024]{1,0:T(8,128)(2,1)S(1)}, bf16[128,1024]{1,0:T(8,128)(2,1)S(1)}) custom-call(s32[8]{0:T(128)S(1)} %select_reduce_fusion.5.src, s32[16]{0:T(128)S(1)} %mul.76.okr, s32[1]{0:T(128)} %bitcast.11.ce, bf16[32,256,256]{2,1,0:T(8,128)(2,1)} %all-to-all-done.refs_0_.refs_1_.refs_2_.refs_3_.refs_4_.refs_5_.refs_6_.refs_7_.a), custom_call_target="tpu_custom_call" | custom-call | tf_op jit(solution)/shard_map/pallas_call | solution.py:75
  149.4 4.0 %collective-permute-start = (bf16[128,1024]{1,0:T(8,128)(2,1)S(1)}, bf16[128,1024]{1,0:T(8,128)(2,1)S(1)}, u32[]{:S(2)}, u32[]{:S(2)}) collective-permute-start(bf16[128,1024]{1,0:T(8,128)(2,1)S(1)} %get-tuple-element.10), channel_id=1, source_target_pairs={{0,32},{32,0},{1,33},{33,1},{2,34},{34,2},{3,35},{35,3},{4,36},{36... | collective-permute-start | bytes 786440 | tf_op jit(solution)/shard_map/ppermute | solution.py:28
  154.6 1.8 collective-permute-start.1
  156.8 6.8 %shard_map.55 = bf16[2,2,4,8,128,128]{5,4,3,2,1,0:T(8,128)(2,1)S(1)} custom-call(s32[64]{0:T(128)S(1)} %select_reduce_fusion.src, s32[128]{0:T(128)S(1)} %mul.72.okr, bf16[32,256,256]{2,1,0:T(8,128)(2,1)} %all-to-all-done.refs_0_.refs_1_.refs_2_.refs_3_.refs_4_.refs_5_.refs_6_.refs_7_.a, ...), custom_call_target="tpu_custom_call" | custom-call | tf_op jit(solution)/shard_map/pallas_call | solution.py:125
  163.6 2.0 copy-done.1
  165.6 5.9 %all-to-all-start.1 = ((bf16[16,8,128,128]{3,2,1,0:T(8,128)(2,1)}), bf16[16,8,128,128]{3,2,1,0:T(8,128)(2,1)}, u32[]{:S(2)}, u32[]{:S(2)}) async-start(bf16[16,8,128,128]{3,2,1,0:T(8,128)(2,1)} %bitcast.56), calls=%async_computation.1 | async-start | bytes 8388608 | tf_op jit(solution)/shard_map/all_to_all | solution.py:286
  173.0 2.1 shard_map.58
  175.2 1.9 collective-permute-start.12
  179.0 1.7 collective-permute-start.6
  181.9 4.5 %collective-permute-done.9 = bf16[128,1536]{1,0:T(8,128)(2,1)S(1)} collective-permute-done((bf16[128,1536]{1,0:T(8,128)(2,1)S(1)}, bf16[128,1536]{1,0:T(8,128)(2,1)S(1)}, u32[]{:S(2)}, u32[]{:S(2)}) %collective-permute-start.9) | collective-permute-done | bytes 393248 | tf_op jit(solution)/shard_map/ppermute | solution.py:24
  188.0 42.9 %collective-permute-done.6 = bf16[128,1536]{1,0:T(8,128)(2,1)S(1)} collective-permute-done((bf16[128,1536]{1,0:T(8,128)(2,1)S(1)}, bf16[128,1536]{1,0:T(8,128)(2,1)S(1)}, u32[]{:S(2)}, u32[]{:S(2)}) %collective-permute-start.6) | collective-permute-done | bytes 393248 | tf_op jit(solution)/shard_map/ppermute | solution.py:24
  230.9 1.9 collective-permute-start.7
  232.8 2.4 collective-permute-start.8
  235.3 1.9 collective-permute-start.14
  237.2 2.3 collective-permute-done.7
  239.7 6.3 %collective-permute-done.14 = bf16[128,1536]{1,0:T(8,128)(2,1)S(1)} collective-permute-done((bf16[128,1536]{1,0:T(8,128)(2,1)S(1)}, bf16[128,1536]{1,0:T(8,128)(2,1)S(1)}, u32[]{:S(2)}, u32[]{:S(2)}) %collective-permute-start.14) | collective-permute-done | bytes 393248 | tf_op jit(solution)/shard_map/ppermute | solution.py:24
  246.8 2.1 collective-permute-start.16
  248.9 2.9 collective-permute-done.15
  252.0 1.7 copy-done.2
  253.7 1.9 copy-done.3
  255.6 7.9 %shard_map.59 = bf16[8,8,64,128]{3,2,1,0:T(8,128)(2,1)S(1)} custom-call(s32[2]{0:T(128)S(1)} %pad_add_fusion.zs, bf16[4,4,8,128,128]{4,3,2,1,0:T(8,128)(2,1)} %bitcast.9.parts_ref, bf16[4,128,1536]{2,1,0:T(8,128)(2,1)S(1)} %pad_maximum_fusion.l_ref, bf16[8,128,1536]{2,1,0:T(8,128)(2,1)S(1)} %copy-done.3), custom_call_target="tpu_custom_call" | custom-call | tf_op jit(solution)/shard_map/pallas_call | solution.py:207
  263.5 21.0 %all_to_all.20.a = bf16[8,8,64,128]{3,2,1,0:T(8,128)(2,1)S(1)} all-to-all(bf16[8,8,64,128]{3,2,1,0:T(8,128)(2,1)S(1)} %shard_map.59), channel_id=1, replica_groups=mesh['q'=2,'yp'=2,'core'=2,'z'=8,'x'=4] {'core','x'}, dimensions={0} | all-to-all | bytes 2097152 | tf_op jit(solution)/shard_map/all_to_all | solution.py:293
  284.5 2.8 shard_map.60
  (98 shorter events, 17.3 us)
Async XLA Ops:
  6.5 150.2 %copy-start = (bf16[4,2,256,256]{3,2,1,0:T(8,128)(2,1)S(1)}, bf16[4,2,256,256]{3,2,1,0:T(8,128)(2,1)}, u32[]{:S(2)}) copy-start(bf16[4,2,256,256]{3,2,1,0:T(8,128)(2,1)} %param.8) | copy-start | bytes 3145732
  12.9 25.7 %all-to-all-start.2 = ((bf16[32,24,256]{2,1,0:T(8,128)(2,1)}), bf16[32,24,256]{2,1,0:T(8,128)(2,1)S(1)}, u32[]{:S(2)}, u32[]{:S(2)}) async-start(bf16[32,24,256]{2,1,0:T(8,128)(2,1)} %broadcast_select_fusion), calls=%async_computation.2 | async-start | bytes 786432 | tf_op jit(solution)/shard_map/all_to_all | solution.py:258
  38.6 106.5 %all-to-all-start = ((bf16[32,256,256]{2,1,0:T(8,128)(2,1)}), bf16[32,256,256]{2,1,0:T(8,128)(2,1)}, u32[]{:S(2)}, u32[]{:S(2)}) async-start(bf16[32,256,256]{2,1,0:T(8,128)(2,1)} %bitcast_select_fusion), calls=%async_computation | async-start | bytes 8388608 | tf_op jit(solution)/shard_map/all_to_all | solution.py:273
  44.6 126.8 %all-gather.2.cloned.1.call-start = ((), (), s32[]{:S(2)}) async-start(), calls=%async_computation.4 | async-start | bytes 2027520 | tf_op jit(solution)/shard_map/all_gather | solution.py:270
  45.8 110.8 %copy-start.5 = (bf16[2,2,256,256]{3,2,1,0:T(8,128)(2,1)S(1)}, bf16[2,2,256,256]{3,2,1,0:T(8,128)(2,1)}, u32[]{:S(2)}) copy-start(bf16[2,2,256,256]{3,2,1,0:T(8,128)(2,1)} %param.9) | copy-start | bytes 1572868
  45.9 2.5 collective-permute-start.2
  48.5 3.3 %collective-permute-start.3 = (bf16[24,768]{1,0:T(8,128)(2,1)S(1)}, bf16[24,768]{1,0:T(8,128)(2,1)S(1)}, u32[]{:S(2)}, u32[]{:S(2)}) collective-permute-start(bf16[24,768]{1,0:T(8,128)(2,1)S(1)} %add_convert_fusion.1), channel_id=1, source_target_pairs={{0,64},{64,0},{1,65},{65,1},{2,66},{66,2},{3,67},{67,3},{4,68},{68... | collective-permute-start | bytes 110600 | tf_op jit(solution)/shard_map/ppermute | solution.py:28
  149.4 5.1 %collective-permute-start = (bf16[128,1024]{1,0:T(8,128)(2,1)S(1)}, bf16[128,1024]{1,0:T(8,128)(2,1)S(1)}, u32[]{:S(2)}, u32[]{:S(2)}) collective-permute-start(bf16[128,1024]{1,0:T(8,128)(2,1)S(1)} %get-tuple-element.10), channel_id=1, source_target_pairs={{0,32},{32,0},{1,33},{33,1},{2,34},{34,2},{3,35},{35,3},{4,36},{36... | collective-permute-start | bytes 786440 | tf_op jit(solution)/shard_map/ppermute | solution.py:28
  154.6 16.9 %collective-permute-start.1 = (bf16[128,1024]{1,0:T(8,128)(2,1)S(1)}, bf16[128,1024]{1,0:T(8,128)(2,1)S(1)}, u32[]{:S(2)}, u32[]{:S(2)}) collective-permute-start(bf16[128,1024]{1,0:T(8,128)(2,1)S(1)} %add_convert_fusion.a_ref), channel_id=1, source_target_pairs={{0,64},{64,0},{1,65},{65,1},{2,66},{66,2},{3,67},{67,3},{4,68},{68... | collective-permute-start | bytes 786440 | tf_op jit(solution)/shard_map/ppermute | solution.py:28
  163.6 2.0 copy-start.1
  165.6 88.1 %all-to-all-start.1 = ((bf16[16,8,128,128]{3,2,1,0:T(8,128)(2,1)}), bf16[16,8,128,128]{3,2,1,0:T(8,128)(2,1)}, u32[]{:S(2)}, u32[]{:S(2)}) async-start(bf16[16,8,128,128]{3,2,1,0:T(8,128)(2,1)} %bitcast.56), calls=%async_computation.1 | async-start | bytes 8388608 | tf_op jit(solution)/shard_map/all_to_all | solution.py:286
  171.5 1.5 copy-start.4
  175.1 11.4 %collective-permute-start.9 = (bf16[128,1536]{1,0:T(8,128)(2,1)S(1)}, bf16[128,1536]{1,0:T(8,128)(2,1)S(1)}, u32[]{:S(2)}, u32[]{:S(2)}) collective-permute-start(bf16[128,1536]{1,0:T(8,128)(2,1)S(1)} %get-tuple-element.12), channel_id=1, source_target_pairs={{0,28},{4,0},{8,4},{12,8},{16,12},{20,16},{24,20},{28,24},{1,29},{... | collective-permute-start | bytes 1179656 | tf_op jit(solution)/shard_map/ppermute | solution.py:24
  175.2 12.1 %collective-permute-start.12 = (bf16[128,1536]{1,0:T(8,128)(2,1)S(1)}, bf16[128,1536]{1,0:T(8,128)(2,1)S(1)}, u32[]{:S(2)}, u32[]{:S(2)}) collective-permute-start(bf16[128,1536]{1,0:T(8,128)(2,1)S(1)} %get-tuple-element.12), channel_id=1, source_target_pairs={{0,4},{4,8},{8,12},{12,16},{16,20},{20,24},{24,28},{28,0},{1,5},{5... | collective-permute-start | bytes 1179656 | tf_op jit(solution)/shard_map/ppermute | solution.py:24
  177.1 1.8 collective-permute-start.4
  179.0 51.9 %collective-permute-start.6 = (bf16[128,1536]{1,0:T(8,128)(2,1)S(1)}, bf16[128,1536]{1,0:T(8,128)(2,1)S(1)}, u32[]{:S(2)}, u32[]{:S(2)}) collective-permute-start(bf16[128,1536]{1,0:T(8,128)(2,1)S(1)} %broadcast_select_fusion.1), channel_id=1, source_target_pairs={{0,1},{1,2},{2,3},{3,0},{4,5},{5,6},{6,7},{7,4},{8,9},{9,10},{10,1... | collective-permute-start | bytes 1179656 | tf_op jit(solution)/shard_map/ppermute | solution.py:24
  180.6 52.2 %collective-permute-start.5 = (bf16[128,1536]{1,0:T(8,128)(2,1)S(1)}, bf16[128,1536]{1,0:T(8,128)(2,1)S(1)}, u32[]{:S(2)}, u32[]{:S(2)}) collective-permute-start(bf16[128,1536]{1,0:T(8,128)(2,1)S(1)} %broadcast_select_fusion.1), channel_id=1, source_target_pairs={{0,3},{1,0},{2,1},{3,2},{4,7},{5,4},{6,5},{7,6},{8,11},{9,8},{10,9... | collective-permute-start | bytes 1179656 | tf_op jit(solution)/shard_map/ppermute | solution.py:24
  186.5 48.7 %collective-permute-start.10 = (bf16[128,1536]{1,0:T(8,128)(2,1)S(1)}, bf16[128,1536]{1,0:T(8,128)(2,1)S(1)}, u32[]{:S(2)}, u32[]{:S(2)}) collective-permute-start(bf16[128,1536]{1,0:T(8,128)(2,1)S(1)} %collective-permute-done.9), channel_id=1, source_target_pairs={{0,28},{4,0},{8,4},{12,8},{16,12},{20,16},{24,20},{28,24},{1,29},{... | collective-permute-start | bytes 1179656 | tf_op jit(solution)/shard_map/ppermute | solution.py:24
  187.3 48.0 %collective-permute-start.13 = (bf16[128,1536]{1,0:T(8,128)(2,1)S(1)}, bf16[128,1536]{1,0:T(8,128)(2,1)S(1)}, u32[]{:S(2)}, u32[]{:S(2)}) collective-permute-start(bf16[128,1536]{1,0:T(8,128)(2,1)S(1)} %collective-permute-done.12), channel_id=1, source_target_pairs={{0,4},{4,8},{8,12},{12,16},{16,20},{20,24},{24,28},{28,0},{1,5},{5... | collective-permute-start | bytes 1179656 | tf_op jit(solution)/shard_map/ppermute | solution.py:24
  230.9 8.6 %collective-permute-start.7 = (bf16[64,1536]{1,0:T(8,128)(2,1)S(1)}, bf16[64,1536]{1,0:T(8,128)(2,1)S(1)}, u32[]{:S(2)}, u32[]{:S(2)}) collective-permute-start(bf16[64,1536]{1,0:T(8,128)(2,1)S(1)} %slice.54), channel_id=1, source_target_pairs={{0,1},{1,2},{2,3},{3,0},{4,5},{5,6},{6,7},{7,4},{8,9},{9,10},{10,1... | collective-permute-start | bytes 589832 | tf_op jit(solution)/shard_map/ppermute | solution.py:24
  232.8 6.7 %collective-permute-start.8 = (bf16[64,1536]{1,0:T(8,128)(2,1)S(1)}, bf16[64,1536]{1,0:T(8,128)(2,1)S(1)}, u32[]{:S(2)}, u32[]{:S(2)}) collective-permute-start(bf16[64,1536]{1,0:T(8,128)(2,1)S(1)} %slice.55), channel_id=1, source_target_pairs={{0,3},{1,0},{2,1},{3,2},{4,7},{5,4},{6,5},{7,6},{8,11},{9,8},{10,9... | collective-permute-start | bytes 589832 | tf_op jit(solution)/shard_map/ppermute | solution.py:24
  235.2 11.5 %collective-permute-start.11 = (bf16[128,1536]{1,0:T(8,128)(2,1)S(1)}, bf16[128,1536]{1,0:T(8,128)(2,1)S(1)}, u32[]{:S(2)}, u32[]{:S(2)}) collective-permute-start(bf16[128,1536]{1,0:T(8,128)(2,1)S(1)} %collective-permute-done.10), channel_id=1, source_target_pairs={{0,28},{4,0},{8,4},{12,8},{16,12},{20,16},{24,20},{28,24},{1,29},{... | collective-permute-start | bytes 1179656 | tf_op jit(solution)/shard_map/ppermute | solution.py:24
  235.3 10.7 %collective-permute-start.14 = (bf16[128,1536]{1,0:T(8,128)(2,1)S(1)}, bf16[128,1536]{1,0:T(8,128)(2,1)S(1)}, u32[]{:S(2)}, u32[]{:S(2)}) collective-permute-start(bf16[128,1536]{1,0:T(8,128)(2,1)S(1)} %collective-permute-done.13), channel_id=1, source_target_pairs={{0,4},{4,8},{8,12},{12,16},{16,20},{20,24},{24,28},{28,0},{1,5},{5... | collective-permute-start | bytes 1179656 | tf_op jit(solution)/shard_map/ppermute | solution.py:24
  246.0 5.8 %collective-permute-start.15 = (bf16[64,1536]{1,0:T(8,128)(2,1)S(1)}, bf16[64,1536]{1,0:T(8,128)(2,1)S(1)}, u32[]{:S(2)}, u32[]{:S(2)}) collective-permute-start(bf16[64,1536]{1,0:T(8,128)(2,1)S(1)} %slice.56), channel_id=1, source_target_pairs={{0,4},{4,8},{8,12},{12,16},{16,20},{20,24},{24,28},{28,0},{1,5},{5... | collective-permute-start | bytes 589832 | tf_op jit(solution)/shard_map/ppermute | solution.py:24
  246.8 5.1 %collective-permute-start.16 = (bf16[64,1536]{1,0:T(8,128)(2,1)S(1)}, bf16[64,1536]{1,0:T(8,128)(2,1)S(1)}, u32[]{:S(2)}, u32[]{:S(2)}) collective-permute-start(bf16[64,1536]{1,0:T(8,128)(2,1)S(1)} %slice.57), channel_id=1, source_target_pairs={{0,28},{4,0},{8,4},{12,8},{16,12},{20,16},{24,20},{28,24},{1,29},{... | collective-permute-start | bytes 589832 | tf_op jit(solution)/shard_map/ppermute | solution.py:24
  252.0 1.7 copy-start.2
  253.7 1.9 copy-start.3
Sparse Core Ops, SparseCore 0:
  52.6 99.9 all-gather.1

commit v2 on v1

v2 whole, which is shorter than its diff:
```python
import jax
import jax.numpy as jnp
from jax import lax
from jax.experimental import pallas as pl
from jax.experimental.pallas import tpu as pltpu
from jax.sharding import Mesh, PartitionSpec as P

BLOCK = 128
PANEL = 256
NB = 64
NZ = 8
NX = 4
HALF = NB // 2
BF = jnp.bfloat16
F32 = jnp.float32
VMEM = 24 * 1024 * 1024
LARGE = 56 * 1024 * 1024


def params(limit=VMEM):
    return pltpu.CompilerParams(vmem_limit_bytes=limit)


def cost(us):
    return pl.CostEstimate(flops=0, bytes_accessed=int(us * 3.6e5), transcendentals=0)


def shift(v, axis, step, n):
    return lax.ppermute(v, axis, [(i, (i + step) % n) for i in range(n)])


def flip(v, axis):
    return lax.ppermute(v, axis, [(0, 1), (1, 0)])


ANY = pl.BlockSpec(memory_space=pl.ANY)


def tie(values, *earlier):
    n = len(values)
    return pl.pallas_call(
        lambda *refs: None,
        out_shape=tuple(jax.ShapeDtypeStruct(v.shape, v.dtype) for v in values),
        in_specs=[ANY] * (n + len(earlier)),
        out_specs=(ANY,) * n,
        cost_estimate=cost(0.5),
        input_output_aliases={i: i for i in range(n)},
    )(*values, *earlier)


def both_ways(pair, axis, n):
    return shift(pair[0], axis, 1, n), shift(pair[1], axis, -1, n)


def onehot_pick(table, index):
    hit = index[:, None] == jnp.arange(table.shape[0], dtype=jnp.int32)[None, :]
    return jnp.sum(jnp.where(hit, table[None, :], 0), axis=1).astype(jnp.int32)


def block_maps(child_row, merged_row):
    target = jnp.arange(NB, dtype=jnp.int32)
    hits = merged_row[None, :] == target[:, None]
    filled = jnp.any(hits, axis=1)
    place = jnp.sum(jnp.where(hits, jnp.arange(merged_row.shape[0], dtype=jnp.int32)[None, :] + 4, 0), axis=1)
    before = target[None, :] < target[:, None]
    rank = jnp.sum(jnp.where(before & ~filled[None, :], 1, 0), axis=1)
    first_index = jnp.where(filled, place, rank).astype(jnp.int32)
    child_hits = child_row[None, :] == first_index[:, None]
    source = jnp.sum(jnp.where(child_hits, target[None, :], 0), axis=1).astype(jnp.int32)
    wanted = jnp.arange(4, dtype=jnp.int32)
    pivot = (~filled)[None, :] & (rank[None, :] == wanted[:, None])
    pivot_places = jnp.sum(jnp.where(pivot, target[None, :], 0), axis=1).astype(jnp.int32)
    return source, filled.astype(jnp.int32), pivot_places


def panel_blocks(rows, source, ok, core, *earlier):
    def body(src, okr, ce, *refs):
        e = ce[0]
        for i in range(8):
            for out, r in ((refs[-2], e), (refs[-1], 1 - e)):
                part = refs[i][0, pl.ds(pl.multiple_of(r * BLOCK, BLOCK), BLOCK), :]
                out[:, i * BLOCK:(i + 1) * BLOCK] = jnp.where(okr[i * 2 + r] > 0, part, jnp.zeros_like(part))

    def where_from(i):
        return lambda g, s, o, c: (s[i] // 2, 0, s[i] % 2)
    one = jax.ShapeDtypeStruct((BLOCK, 8 * BLOCK), BF)
    return pl.pallas_call(
        body,
        out_shape=(one, one),
        grid_spec=pltpu.PrefetchScalarGridSpec(
            num_scalar_prefetch=3,
            grid=(1,),
            in_specs=[pl.BlockSpec((1, 2 * BLOCK, BLOCK), where_from(i)) for i in range(8)] + [ANY] * len(earlier),
            out_specs=[pl.BlockSpec((BLOCK, 8 * BLOCK), lambda g, s, o, c: (0, 0))] * 2,
        ),
        cost_estimate=cost(1.8),
        compiler_params=params(),
    )(source, ok, core, *[rows] * 8, *earlier)


def core_send(rows, source, core, *earlier):
    def body(src, ce, rows_ref, *refs):
        far, held, sems, out_sems = refs[-4:]
        ins, outs = [], []
        for x in range(NX):
            for z in range(NZ):
                b = src[2 * (z * NX + x) + 1 - ce[0]]
                lanes = pl.ds(pl.multiple_of(b % 2 * BLOCK, BLOCK), BLOCK)
                ins.append(pltpu.make_async_copy(rows_ref.at[b // 2, :, lanes], held.at[x, z], sems.at[x, z]))
                ins[-1].start()
        for x in range(NX):
            for z in range(NZ):
                ins[x * NZ + z].wait()
            outs.append(pltpu.make_async_copy(held.at[x], far.at[x], out_sems.at[x]))
            outs[-1].start()
        for move in outs:
            move.wait()

    shape = (NX, NZ, 2 * BLOCK, BLOCK)
    return pl.pallas_call(
        body,
        out_shape=jax.ShapeDtypeStruct(shape, BF),
        grid_spec=pltpu.PrefetchScalarGridSpec(
            num_scalar_prefetch=2,
            grid=(1,),
            in_specs=[ANY] * (1 + len(earlier)),
            out_specs=ANY,
            scratch_shapes=[
                pltpu.VMEM(shape, BF),
                pltpu.SemaphoreType.DMA((NX, NZ)),
                pltpu.SemaphoreType.DMA((NX,)),
            ],
        ),
        cost_estimate=cost(3.3),
        compiler_params=params(),
    )(source, core, rows, *earlier)


def pick_rows(slab, source):
    n = source.shape[0]

    def body(src, *refs):
        for i in range(n):
            refs[-1][i] = refs[i][0]
    shape = (n,) + slab.shape[1:]

    def where_from(i):
        return lambda g, s: (s[i], 0, 0)
    return pl.pallas_call(
        body,
        out_shape=jax.ShapeDtypeStruct(shape, BF),
        grid_spec=pltpu.PrefetchScalarGridSpec(
            num_scalar_prefetch=1,
            grid=(1,),
            in_specs=[pl.BlockSpec((1,) + slab.shape[1:], where_from(i)) for i in range(n)],
            out_specs=pl.BlockSpec(shape, lambda g, s: (0, 0, 0)),
        ),
        cost_estimate=cost(1.3),
        compiler_params=params(),
    )(source, *[slab] * n)


def few_blocks(rows, source):
    few = rows.shape[1]

    def body(src, *refs):
        for i in range(6):
            refs[-1][:, i * BLOCK:(i + 1) * BLOCK] = refs[i][0]

    def where_from(i):
        return lambda g, s: (s[i] // 2, 0, s[i] % 2)
    return pl.pallas_call(
        body,
        out_shape=jax.ShapeDtypeStruct((few, 6 * BLOCK), BF),
        grid_spec=pltpu.PrefetchScalarGridSpec(
            num_scalar_prefetch=1,
            grid=(1,),
            in_specs=[pl.BlockSpec((1, few, BLOCK), where_from(i)) for i in range(6)],
            out_specs=pl.BlockSpec((few, 6 * BLOCK), lambda g, s: (0, 0)),
        ),
        cost_estimate=cost(0.6),
        compiler_params=params(),
    )(source, *[rows] * 6)


STEP = NZ


def column_specs(core_of):
    def where_from(i):
        def index(x, w, s, o, c):
            b = s[2 * ((w * STEP + i) * NX + x) + core_of(c[0])]
            return (b // 2, 0, b % 2)
        return index
    return [pl.BlockSpec((1, 2 * BLOCK, BLOCK), where_from(i)) for i in range(STEP)]


def core_sum(rows, got, source, ok, place):
    def body(src, okr, ce, *refs):
        x, w = pl.program_id(0), pl.program_id(1)
        keep, send = refs[-2:]
        for i in range(STEP):
            c = 2 * ((w * STEP + i) * NX + x) + ce[0]
            for out, r in ((keep, ce[1]), (send, 1 - ce[1])):
                part = pl.ds(pl.multiple_of(r * BLOCK, BLOCK), BLOCK)
                total = (refs[i][0, part, :].astype(F32) + refs[STEP][0, i, part, :].astype(F32)).astype(BF)
                out[0, i] = jnp.where(okr[c * 2 + r] > 0, total, jnp.zeros_like(total))

    one = jax.ShapeDtypeStruct((NX, NZ, BLOCK, BLOCK), BF)
    return pl.pallas_call(
        body,
        out_shape=(one, one),
        grid_spec=pltpu.PrefetchScalarGridSpec(
            num_scalar_prefetch=3,
            grid=(NX, NZ // STEP),
            in_specs=column_specs(lambda e: e) + [
                pl.BlockSpec((1, STEP, 2 * BLOCK, BLOCK), lambda x, w, s, o, c: (x, w, 0, 0))],
            out_specs=[pl.BlockSpec((1, STEP, BLOCK, BLOCK), lambda x, w, s, o, c: (x, w, 0, 0))] * 2,
        ),
        cost_estimate=cost(4.2),
        compiler_params=params(),
    )(source, ok, place, *[rows] * STEP, got)


def mm(a, b):
    return jnp.dot(a, b, preferred_element_type=F32)


def mm_t(a, b):
    return lax.dot_general(a, b, (((1,), (1,)), ((), ())), preferred_element_type=F32)


def lead_rows(special, w_one, place):
    n = PANEL

    def body(y, s_ref, w1, t_out, lead_out):
        lead = s_ref[2 * n:, 4 * n:].astype(F32)
        for p in range(2):
            low = slice(2 * p * n, (2 * p + 1) * n)
            high = slice((2 * p + 1) * n, (2 * p + 2) * n)
            t0 = s_ref[n:, low]
            l0 = mm(t0, w1[p, 0]).astype(BF)
            t1 = (s_ref[n:, high].astype(F32) - mm_t(l0, s_ref[:n, low])).astype(BF)
            l1 = mm(t1[n:], w1[p, 1]).astype(BF)
            lead = lead - mm_t(l0[n:], t0[:n]) - mm_t(l1, t1[:n])
            t_out[:, low] = t0
            t_out[:, high] = t1
        lead_out[...] = lead.astype(BF)

    def whole(v):
        return pl.BlockSpec(v.shape, lambda g, y: (0, 0))
    out = jax.ShapeDtypeStruct((2 * n, 4 * n), BF), jax.ShapeDtypeStruct((n, n), BF)
    return pl.pallas_call(
        body,
        out_shape=out,
        grid_spec=pltpu.PrefetchScalarGridSpec(
            num_scalar_prefetch=1,
            grid=(1,),
            in_specs=[whole(special), pl.BlockSpec((2, 2, n, n), lambda g, y: (y[1], 0, 0, 0))],
            out_specs=[whole(v) for v in out],
        ),
        cost_estimate=cost(1.6),
        compiler_params=params(),
    )(place, special, w_one)


def factor_rows(mine, other, special, lead, w_one, w_two, place, *earlier):
    n = PANEL

    def body(y, a_ref, b_ref, p0, p1, t_ref, lead_ref, w1, w2, *refs):
        c_out, l_out = refs[-2:]
        first = y[0] == 0
        a, b = a_ref[...], b_ref[...]
        both = (jnp.where(first, a, b), jnp.where(first, b, a))
        panel = (a[:, 2 * n:].astype(F32) + b[:, 2 * n:].astype(F32)).astype(BF).astype(F32)
        for p in range(2):
            low = slice(2 * p * n, (2 * p + 1) * n)
            high = slice((2 * p + 1) * n, (2 * p + 2) * n)
            c0 = both[p][:, :n]
            l0 = mm(c0, w1[p, 0]).astype(BF)
            c1 = (both[p][:, n:2 * n].astype(F32) - mm_t(l0, (p0, p1)[p][...])).astype(BF)
            l1 = mm(c1, w1[p, 1]).astype(BF)
            panel = panel - mm_t(l0, t_ref[:, low]) - mm_t(l1, t_ref[:, high])
            c_out[:, p * n:(p + 1) * n] = c1
            l_out[:, p * n:(p + 1) * n] = l0
            l_out[:, (2 + p) * n:(3 + p) * n] = l1
        d0 = panel[:, :n].astype(BF)
        k0 = mm(d0, w2[0, 0]).astype(BF)
        d1 = (panel[:, n:] - mm_t(k0, lead_ref[...])).astype(BF)
        c_out[:, 2 * n:3 * n] = d0
        c_out[:, 3 * n:] = d1
        l_out[:, 4 * n:5 * n] = k0
        l_out[:, 5 * n:] = mm(d1, w2[0, 1]).astype(BF)

    def whole(v):
        return pl.BlockSpec(v.shape, lambda g, y: (0, 0))
    out = [jax.ShapeDtypeStruct((BLOCK, k * n), BF) for k in (4, 6)]
    return pl.pallas_call(
        body,
        out_shape=out,
        grid_spec=pltpu.PrefetchScalarGridSpec(
            num_scalar_prefetch=1,
            grid=(1,),
            in_specs=[
                whole(mine), whole(other),
                pl.BlockSpec((n, n), lambda g, y: (0, 0)),
                pl.BlockSpec((n, n), lambda g, y: (0, 2)),
                whole(lead[0]), whole(lead[1]),
                pl.BlockSpec((2, 2, n, n), lambda g, y: (y[1], 0, 0, 0)),
                pl.BlockSpec((1, 2, n, n), lambda g, y: (y[1], 0, 0, 0)),
            ] + [ANY] * len(earlier),
            out_specs=[whole(v) for v in out],
        ),
        cost_estimate=cost(3.5),
        compiler_params=params(),
    )(place, mine, other, special, special, *lead, w_one, w_two, *earlier)


def tile_update(parts, lower, first, columns, place):
    half = BLOCK // 2
    deep = first.shape[-1]

    def body(zs, *refs):
        part, head, l_refs, c_refs = refs[:2], refs[2:4], refs[4:4 + NX], refs[4 + NX:4 + NX + NZ]
        out, low = refs[-2:]

        @pl.when(pl.program_id(0) == 0)
        def _():
            for i in range(NX):
                low[pl.ds(pl.multiple_of((zs[1] + i) % NX * BLOCK, BLOCK), BLOCK), :] = l_refs[i][...]

        for step in range(NZ // 2):
            @pl.when(pl.program_id(0) == step)
            def _():
                c = jnp.concatenate([c_refs[2 * step][...], c_refs[2 * step + 1][...]], axis=0)
                update = mm_t(low[:, deep:], c) + mm_t(low[:, :deep], jnp.concatenate([head[0][0], head[1][0]], axis=0))
                for j in range(2):
                    for x in range(NX):
                        rows = slice(x * BLOCK, (x + 1) * BLOCK)
                        done = (part[j][x, 0].astype(F32) - update[rows, j * BLOCK:(j + 1) * BLOCK]).astype(BF)
                        out[x, j] = done[:half]
                        out[NX + x, j] = done[half:]

    def part_spec(j):
        return pl.BlockSpec((NX, 1, BLOCK, BLOCK), lambda g, s: (0, (s[0] + 2 * g + j) % NZ, 0, 0))

    def head_spec(j):
        return pl.BlockSpec((1, BLOCK, deep), lambda g, s: ((s[0] + 2 * g + j) % NZ, 0, 0))

    def whole(v):
        return pl.BlockSpec(v.shape, lambda g, s: (0, 0))
    return pl.pallas_call(
        body,
        out_shape=jax.ShapeDtypeStruct((2 * NX, NZ, half, BLOCK), BF),
        grid_spec=pltpu.PrefetchScalarGridSpec(
            num_scalar_prefetch=1,
            grid=(NZ // 2,),
            in_specs=[part_spec(0), part_spec(1), head_spec(0), head_spec(1)] + [whole(v) for v in (*lower, *columns)],
            out_specs=pl.BlockSpec((2 * NX, 2, half, BLOCK), lambda g, s: (0, g, 0, 0)),
            scratch_shapes=[pltpu.VMEM((NX * BLOCK, lower[0].shape[1]), BF)],
        ),
        cost_estimate=cost(7),
        compiler_params=params(LARGE),
    )(place, parts, parts, first, first, *lower, *columns)


def join_rows(pieces, place):
    half = BLOCK // 2
    wide = 2 * NX * BLOCK
    some = NZ // 2

    def body(zs, *refs):
        for i in range(some):
            for k in range(2):
                for x in range(NX):
                    c = i * wide + (2 * x + k) * BLOCK
                    refs[-1][:, c:c + BLOCK] = refs[i][k * NX + x, 0]

    def where_from(i):
        return lambda g, s: (0, (g * some + i + NZ - s[0]) % NZ, 0, 0)
    return pl.pallas_call(
        body,
        out_shape=jax.ShapeDtypeStruct((half, NB * BLOCK), BF),
        grid_spec=pltpu.PrefetchScalarGridSpec(
            num_scalar_prefetch=1,
            grid=(NZ // some,),
            in_specs=[pl.BlockSpec((2 * NX, 1, half, BLOCK), where_from(i)) for i in range(some)],
            out_specs=pl.BlockSpec((half, some * wide), lambda g, s: (0, g)),
        ),
        cost_estimate=cost(2.2),
        compiler_params=params(),
    )(place, *[pieces] * some)


def local(child_blocks, child_map, merged_map, pivots_one, pivots_two):
    q, yp, e = lax.axis_index("q"), lax.axis_index("yp"), lax.axis_index("core")
    z, x = lax.axis_index("z"), lax.axis_index("x")
    child = (q * 2 + yp) * 2 + e
    spot = z * NX + x
    slab = child_blocks[0].reshape(NB, BLOCK, 2 * BLOCK)
    source, filled, pivot_places = block_maps(child_map[child], merged_map[child // 2])

    own_filled = lax.dynamic_slice_in_dim(filled, 2 * spot, 2)
    lead_filled = filled[:4]
    panel_src = onehot_pick(source, jnp.concatenate([pivot_places, jnp.arange(4, dtype=jnp.int32)]))
    col_ok = jnp.concatenate([jnp.ones((4,), jnp.int32), lead_filled])

    row_src = onehot_pick(source, jnp.concatenate([pivot_places[2:], jnp.arange(4, dtype=jnp.int32)]))
    few = 6 * BLOCK // (NZ * NX)
    first = pick_rows(slab, row_src).reshape(NZ * NX, few, 2 * BLOCK)
    first = lax.all_to_all(first, ("z", "x"), split_axis=0, concat_axis=0, tiled=True)
    part_of = (spot * few + jnp.arange(few, dtype=jnp.int32)) // BLOCK
    row_ok = onehot_pick(jnp.concatenate([jnp.ones((2,), jnp.int32), lead_filled]), part_of)
    first = few_blocks(first, panel_src)
    first_ok = (row_ok[:, None] * jnp.repeat(col_ok, BLOCK)[None, :6 * BLOCK]) > 0
    first = jnp.where(first_ok, first, jnp.zeros_like(first))
    first = (first.astype(F32) + flip(first, "core").astype(F32)).astype(BF)
    second = flip(first, "yp")
    low = jnp.where(yp == 0, first, second)
    high = jnp.where(yp == 0, second, first)
    lead = (low[:, 2 * PANEL:].astype(F32) + high[:, 2 * PANEL:].astype(F32)).astype(BF)
    special = jnp.concatenate([low[:, :2 * PANEL], high[:, :2 * PANEL], lead], axis=1)
    special = lax.all_gather(special, ("z", "x"), axis=0, tiled=True)

    sent = slab.at[source].get(mode="promise_in_bounds").reshape(NZ * NX, 2 * BLOCK, 2 * BLOCK)
    rows = lax.all_to_all(sent, ("z", "x"), split_axis=0, concat_axis=0, tiled=True)

    panel_ok = (col_ok[:, None] * own_filled[None, :]).reshape(-1)
    core = e.reshape(1)
    tile_ok = (filled[:, None] * own_filled[None, :]).reshape(-1)
    group = jnp.stack([yp, q])
    lead = lead_rows(special, pivots_one, group)
    keep, send = panel_blocks(rows, panel_src, panel_ok, core, *lead)
    mine = (keep.astype(F32) + flip(send, "core").astype(F32)).astype(BF)
    other = flip(mine, "yp")
    tile_got = flip(core_send(rows, source, core, mine), "core")
    first = jnp.concatenate([
        jnp.where(yp == 0, mine, other)[:, :PANEL], jnp.where(yp == 0, other, mine)[:, :PANEL]], axis=1)
    first = lax.all_gather(first, "z", axis=0, tiled=False)
    own, theirs = core_sum(rows, tile_got, source, tile_ok, jnp.stack([e, yp]))
    columns, lower = factor_rows(mine, other, special, lead, pivots_one, pivots_two, group, own)

    place = jnp.stack([z, x])
    z1 = tie(both_ways((columns, columns), "z", NZ))
    mate = flip(lower, "core")
    lower = jnp.where(e == yp, lower, mate)
    x1 = tie(both_ways((lower, lower), "x", NX))
    parts = (own.astype(F32) + flip(theirs, "yp").astype(F32)).astype(BF)
    x2 = shift(x1[0], "x", 1, NX)
    parts, = tie((parts,), x2)
    parts = lax.all_to_all(parts, "x", split_axis=0, concat_axis=0, tiled=True)
    z2 = tie(both_ways(z1, "z", NZ))
    z3 = tie(both_ways(z2, "z", NZ))
    z4 = shift(z3[0], "z", 1, NZ)
    lower = (lower, x1[1], x2, x1[0])

    columns = (columns, z1[1], z2[1], z3[1], z4, z3[0], z2[0], z1[0])
    done = tile_update(parts, lower, first, columns, place)
    done = lax.all_to_all(done, ("core", "x"), split_axis=0, concat_axis=0, tiled=True)
    return join_rows(done, place)[None, None]


def solution(mesh):
    fine = Mesh(mesh.devices.reshape(2, 2, 2, NZ, NX), ("q", "yp", "core", "z", "x"))
    leaf, plane = ("q", "yp", "core"), ("z", "x")
    return jax.shard_map(
        local,
        mesh=fine,
        in_specs=(P(leaf, None, plane), P(), P(), P(), P()),
        out_specs=P(plane, leaf, None, None),
        check_vma=False,
    )
```

time: 295 us -> 263 us (0.89)
  waiting for transfers between devices: 160 us -> 136 us
  starting transfers between devices: 48.5 us -> 42.1 us
    all_gather x1, waiting for transfers between devices: 0.01 us -> 96.2 us  [local(): special = lax.all_gather(special, ('z', 'x'), axis=0, tiled=True)]
    all_to_all x1, waiting for transfers between devices: 92.4 us -> 0.01 us  [local(): lax.all_to_all(sent, ('z', 'x'), split_axis=0, concat_axis=0, tiled=True)]
    ppermute x12 -> x10, waiting for transfers between devices: 59 us -> 17.4 us  [shift(): return lax.ppermute(v, axis, [(i, (i + step) % n) for i in range(n)])]
    ppermute x5 -> x7, waiting for transfers between devices: 5.19 us -> 13.3 us  [flip(): return lax.ppermute(v, axis, [(0, 1), (1, 0)])]
    pallas_call x2 -> x10, Pallas kernels: 8.88 us -> 14.4 us  [the longest x1 4.56 us: core_sum(): pl.pallas_call(body, out_shape=(one, one), grid_spec=pltpu.PrefetchScalar...]
    all_to_all x1, waiting for transfers between devices: 3.32 us -> 8.75 us  [local(): lax.all_to_all(first, ('z', 'x'), split_axis=0, concat_axis=0, tiled=True)]
    select_n x5 -> x3, other arithmetic: 6.24 us -> 0.95 us  [the longest x1 0.85 us: local(): jnp.where(yp == 0, mine, other)[:, :PANEL]]
    unnamed x19 -> x40, local copies, waits for them, and re-layouts: 7.27 us -> 10.7 us
  transfers between devices with their start and end apart: 21 -> 22, of which waited for: 11 -> 11; matrix products, arithmetic and copies ran while one was open for 4% -> 4% of each run, Pallas kernels for 5% -> 3%
where the time goes in v2:
time: 263 us; the launch traced here: 262 us
  waiting for transfers between devices  136 us (52%)
  starting transfers between devices  42.1 us (16%)
  Pallas kernels  25.7 us (10%)
  blocking collectives  22.1 us (8%)
  local copies, waits for them, and re-layouts  17 us (6%)
  between operations  13.7 us (5%)
  other arithmetic  6.03 us (2%)
    all_gather x1, waiting for transfers between devices, local(): special = lax.all_gather(special, ('z', 'x'), axis=0, tiled=True)  96.2 us
    all_to_all x1, blocking collectives, local(): lax.all_to_all(done, ('core', 'x'), split_axis=0, concat_axis=0, tiled=True)  22.1 us
    ppermute x10, waiting for transfers between devices, shift(): return lax.ppermute(v, axis, [(i, (i + step) % n) for i in range(n)])  17.4 us
    ppermute x7, waiting for transfers between devices, flip(): return lax.ppermute(v, axis, [(0, 1), (1, 0)])  13.3 us
    ppermute x10, starting transfers between devices, shift(): return lax.ppermute(v, axis, [(i, (i + step) % n) for i in range(n)])  12.9 us
    all_to_all x1, starting transfers between devices, local(): lax.all_to_all(first, ('z', 'x'), split_axis=0, concat_axis=0, tiled=True)  11.9 us
    unnamed x40, local copies, waits for them, and re-layouts  10.7 us
    all_to_all x1, waiting for transfers between devices, local(): lax.all_to_all(first, ('z', 'x'), split_axis=0, concat_axis=0, tiled=True)  8.75 us
  transfers between devices with their start and end apart: 22, of which 11 were waited for; matrix products, arithmetic and copies ran while one was open for 4% of the time, Pallas kernels for 3%

profile of v2, /device:TPU:1, one launch (start us, length us, event | category | flops | bytes accessed | tf_op | source)
XLA Modules:
  0.0 262.4 jit_solution(6490132917966971335)
XLA Ops:
  8.3 2.2 copy-done.1
  10.5 1.3 shard_map.55
  11.8 11.9 %all-to-all-start.1 = ((bf16[32,24,256]{2,1,0:T(8,128)(2,1)}), bf16[32,24,256]{2,1,0:T(8,128)(2,1)S(1)}, u32[]{:S(2)}, u32[]{:S(2)}) async-start(bf16[32,24,256]{2,1,0:T(8,128)(2,1)} %bitcast.12), calls=%async_computation.1 | async-start | bytes 786432 | tf_op jit(solution)/shard_map/all_to_all | solution.py:411
  23.7 5.0 %gather_fusion = bf16[64,128,256]{2,1,0:T(8,128)(2,1)} fusion(bf16[64,128,256]{2,1,0:T(8,128)(2,1)} %bitcast.21, s32[1024]{0:T(1024)S(1)} %pad_clamp_fusion), kind=kCustom, calls=%fused_computation | custom fusion | bytes 8388864 | tf_op jit(solution)/shard_map/gather | solution.py:425
  28.7 8.8 %all-to-all-done.1.refs_0_.refs_1_.refs_2_.refs_3_.refs_4_.refs_5_ = bf16[32,24,256]{2,1,0:T(8,128)(2,1)S(1)} async-done(((bf16[32,24,256]{2,1,0:T(8,128)(2,1)}), bf16[32,24,256]{2,1,0:T(8,128)(2,1)S(1)}, u32[]{:S(2)}, u32[]{:S(2)}) %all-to-all-start.1) | async-done | bytes 393248 | tf_op jit(solution)/shard_map/all_to_all | solution.py:411
  37.5 5.3 %all-to-all-start = ((bf16[32,256,256]{2,1,0:T(8,128)(2,1)}), bf16[32,256,256]{2,1,0:T(8,128)(2,1)}, u32[]{:S(2)}, u32[]{:S(2)}) async-start(bf16[32,256,256]{2,1,0:T(8,128)(2,1)} %bitcast.28), calls=%async_computation | async-start | bytes 8388608 | tf_op jit(solution)/shard_map/all_to_all | solution.py:426
  44.0 2.3 collective-permute-start
  47.2 1.4 collective-permute-start.1
  48.6 1.9 collective-permute-done.1
  51.7 96.2 %all-gather.4.cloned.1.call-done.s_ref.p0.p1 = bf16[768,1280]{1,0:T(8,128)(2,1)} async-done(((bf16[24,1280]{1,0:T(8,128)(2,1)}), bf16[768,1280]{1,0:T(8,128)(2,1)}) %all-gather.4.cloned.1.call-update) | async-done | bytes 1966096 | tf_op jit(solution)/shard_map/all_gather | solution.py:423
  147.9 1.5 copy-done.2
  149.5 1.6 shard_map.57
  151.0 1.8 shard_map.58
  154.8 3.4 %shard_map.59 = bf16[4,8,256,128]{3,2,1,0:T(8,128)(2,1)} custom-call(s32[64]{0:T(128)S(1)} %select_reduce_fusion.src, s32[1]{0:T(128)} %bitcast.4.ce, bf16[32,256,256]{2,1,0:T(8,128)(2,1)} %all-to-all-done.refs_0_.refs_1_.refs_2_.refs_3_.refs_4_.refs_5_.refs_6_.refs_7_.rows_ref, bf16[128,1024]{1,0:T(8,128)(2,1)S(1)} %add_convert_fusion.1.refs_0_.a_ref), custom_call_target="tpu_custom_call" | custom-call | bytes 1188000 | tf_op jit(solution)/shard_map/pallas_call | solution.py:120
  160.1 2.7 %collective-permute-done.3.refs_8_ = bf16[4,8,256,128]{3,2,1,0:T(8,128)(2,1)} collective-permute-done((bf16[4,8,256,128]{3,2,1,0:T(8,128)(2,1)}, bf16[4,8,256,128]{3,2,1,0:T(8,128)(2,1)}, u32[]{:S(2)}, u32[]{:S(2)}) %collective-permute-start.3) | collective-permute-done | bytes 2097184 | tf_op jit(solution)/shard_map/ppermute | solution.py:33
  162.8 4.6 %shard_map.60 = (bf16[4,8,128,128]{3,2,1,0:T(8,128)(2,1)S(1)}, bf16[4,8,128,128]{3,2,1,0:T(8,128)(2,1)S(1)}) custom-call(s32[64]{0:T(128)S(1)} %select_reduce_fusion.src, s32[128]{0:T(128)S(1)} %mul.71.okr, s32[2]{0:T(128)S(1)} %pad_add_fusion.1.ce, ...), custom_call_target="tpu_custom_call" | custom-call | bytes 1512000 | tf_op jit(solution)/shard_map/pallas_call | solution.py:210
  167.4 3.6 %shard_map.61 = (bf16[128,1024]{1,0:T(8,128)(2,1)S(1)}, bf16[128,1536]{1,0:T(8,128)(2,1)}) custom-call(s32[2]{0:T(128)S(1)} %pad_add_fusion.3.y, bf16[128,1024]{1,0:T(8,128)(2,1)S(1)} %add_convert_fusion.1.refs_0_.a_ref, bf16[128,1024]{1,0:T(8,128)(2,1)} %collective-permute-done.5.b_ref, bf16[768,1280]{1,0:T(8,128)(2,1)S(1)} %copy-done.3, ...), custom_call_target="tpu_custom_call" | custom-call | bytes 1260000 | tf_op jit(solution)/shard_map/pallas_call | solution.py:298
  174.9 2.2 collective-permute-start.7
  179.5 1.5 collective-permute-start.11
  180.9 5.2 %collective-permute-done.7.refs_0_ = bf16[128,1536]{1,0:T(8,128)(2,1)S(1)} collective-permute-done((bf16[128,1536]{1,0:T(8,128)(2,1)S(1)}, bf16[128,1536]{1,0:T(8,128)(2,1)S(1)}, u32[]{:S(2)}, u32[]{:S(2)}) %collective-permute-start.7) | collective-permute-done | bytes 393248 | tf_op jit(solution)/shard_map/ppermute | solution.py:29
  189.4 1.9 collective-permute-start.13
  191.3 6.6 %collective-permute-done.4 = bf16[4,8,128,128]{3,2,1,0:T(8,128)(2,1)S(1)} collective-permute-done((bf16[4,8,128,128]{3,2,1,0:T(8,128)(2,1)}, bf16[4,8,128,128]{3,2,1,0:T(8,128)(2,1)S(1)}, u32[]{:S(2)}, u32[]{:S(2)}) %collective-permute-start.4) | collective-permute-done | bytes 1048608 | tf_op jit(solution)/shard_map/ppermute | solution.py:33
  198.0 1.3 add_convert_fusion.refs_0_
  200.1 4.4 %all-to-all-start.2 = ((bf16[4,8,128,128]{3,2,1,0:T(8,128)(2,1)}), bf16[4,8,128,128]{3,2,1,0:T(8,128)(2,1)S(1)}, u32[]{:S(2)}, u32[]{:S(2)}) async-start(bf16[4,8,128,128]{3,2,1,0:T(8,128)(2,1)} %shard_map.63), calls=%async_computation.2 | async-start | bytes 2097152 | tf_op jit(solution)/shard_map/all_to_all | solution.py:451
  205.9 1.2 collective-permute-start.14
  207.1 1.4 collective-permute-start.15
  208.5 6.2 %collective-permute-done.14.refs_0_ = bf16[128,1024]{1,0:T(8,128)(2,1)S(1)} collective-permute-done((bf16[128,1024]{1,0:T(8,128)(2,1)}, bf16[128,1024]{1,0:T(8,128)(2,1)S(1)}, u32[]{:S(2)}, u32[]{:S(2)}) %collective-permute-start.14) | collective-permute-done | bytes 262176 | tf_op jit(solution)/shard_map/ppermute | solution.py:29
  216.1 1.3 collective-permute-start.16
  218.1 5.4 %collective-permute-done.16.refs_12_ = bf16[128,1024]{1,0:T(8,128)(2,1)S(1)} collective-permute-done((bf16[128,1024]{1,0:T(8,128)(2,1)}, bf16[128,1024]{1,0:T(8,128)(2,1)S(1)}, u32[]{:S(2)}, u32[]{:S(2)}) %collective-permute-start.16) | collective-permute-done | bytes 262176 | tf_op jit(solution)/shard_map/ppermute | solution.py:29
  224.6 7.1 %shard_map.67 = bf16[8,8,64,128]{3,2,1,0:T(8,128)(2,1)} custom-call(s32[2]{0:T(128)} %pad_add_fusion.zs, bf16[4,8,128,128]{3,2,1,0:T(8,128)(2,1)} %copy-done.9, bf16[4,8,128,128]{3,2,1,0:T(8,128)(2,1)} %copy-done.9, bf16[8,128,512]{2,1,0:T(8,128)(2,1)} %bitcast.29, bf16[8,128,512]{2,1,0:T(8,128)(2,1)} %bitcast.30, bf16[128,1536]{1,0:T(8,128)(2,1)} %copy-done.13, ...), custom_call_target="tpu_custom_call" | custom-call | bytes 2520000 | tf_op jit(solution)/shard_map/pallas_call | solution.py:352
  231.6 22.1 %all_to_all.20.refs_0_.refs_1_.refs_2_.refs_3_ = bf16[8,8,64,128]{3,2,1,0:T(8,128)(2,1)S(1)} all-to-all(bf16[8,8,64,128]{3,2,1,0:T(8,128)(2,1)} %shard_map.67), channel_id=1, replica_groups=mesh['q'=2,'yp'=2,'core'=2,'z'=8,'x'=4] {'core','x'}, dimensions={0} | all-to-all | bytes 2097152 | tf_op jit(solution)/shard_map/all_to_all | solution.py:459
  253.7 1.8 shard_map.68
  (114 shorter events, 23.6 us)
Async XLA Ops:
  6.5 1.3 copy-start
  8.3 2.2 copy-start.1
  11.8 25.7 %all-to-all-start.1 = ((bf16[32,24,256]{2,1,0:T(8,128)(2,1)}), bf16[32,24,256]{2,1,0:T(8,128)(2,1)S(1)}, u32[]{:S(2)}, u32[]{:S(2)}) async-start(bf16[32,24,256]{2,1,0:T(8,128)(2,1)} %bitcast.12), calls=%async_computation.1 | async-start | bytes 786432 | tf_op jit(solution)/shard_map/all_to_all | solution.py:411
  37.4 110.5 %copy-start.4 = (bf16[4,2,256,256]{3,2,1,0:T(8,128)(2,1)S(1)}, bf16[4,2,256,256]{3,2,1,0:T(8,128)(2,1)}, u32[]{:S(2)}) copy-start(bf16[4,2,256,256]{3,2,1,0:T(8,128)(2,1)} %w1.3) | copy-start | bytes 3145732
  37.5 113.6 %all-to-all-start = ((bf16[32,256,256]{2,1,0:T(8,128)(2,1)}), bf16[32,256,256]{2,1,0:T(8,128)(2,1)}, u32[]{:S(2)}, u32[]{:S(2)}) async-start(bf16[32,256,256]{2,1,0:T(8,128)(2,1)} %bitcast.28), calls=%async_computation | async-start | bytes 8388608 | tf_op jit(solution)/shard_map/all_to_all | solution.py:426
  42.7 105.2 %all-gather.4.cloned.1.call-start = ((), (), s32[]{:S(2)}) async-start(), calls=%async_computation.4 | async-start | bytes 2027520 | tf_op jit(solution)/shard_map/all_gather | solution.py:423
  44.0 3.2 %collective-permute-start = (bf16[24,768]{1,0:T(8,128)(2,1)S(1)}, bf16[24,768]{1,0:T(8,128)(2,1)S(1)}, u32[]{:S(2)}, u32[]{:S(2)}) collective-permute-start(bf16[24,768]{1,0:T(8,128)(2,1)S(1)} %fusion), channel_id=1, source_target_pairs={{0,32},{32,0},{1,33},{33,1},{2,34},{34,2},{3,35},{35,3},{4,36},{36... | collective-permute-start | bytes 110600 | tf_op jit(solution)/shard_map/ppermute | solution.py:33
  47.2 3.3 %collective-permute-start.1 = (bf16[24,768]{1,0:T(8,128)(2,1)S(1)}, bf16[24,768]{1,0:T(8,128)(2,1)S(1)}, u32[]{:S(2)}, u32[]{:S(2)}) collective-permute-start(bf16[24,768]{1,0:T(8,128)(2,1)S(1)} %add_convert_fusion.2), channel_id=1, source_target_pairs={{0,64},{64,0},{1,65},{65,1},{2,66},{66,2},{3,67},{67,3},{4,68},{68... | collective-permute-start | bytes 110600 | tf_op jit(solution)/shard_map/ppermute | solution.py:33
  51.2 166.8 %all-gather.6.cloned.1.call-start = ((), (), s32[]{:S(2)}) async-start(), calls=%async_computation.5 | async-start | bytes 1179648 | tf_op jit(solution)/shard_map/all_gather | solution.py:439
  147.9 1.5 copy-start.2
  152.8 1.9 collective-permute-start.2
  158.2 4.6 %collective-permute-start.3 = (bf16[4,8,256,128]{3,2,1,0:T(8,128)(2,1)}, bf16[4,8,256,128]{3,2,1,0:T(8,128)(2,1)}, u32[]{:S(2)}, u32[]{:S(2)}) collective-permute-start(bf16[4,8,256,128]{3,2,1,0:T(8,128)(2,1)} %shard_map.59), channel_id=1, source_target_pairs={{0,32},{32,0},{1,33},{33,1},{2,34},{34,2},{3,35},{35,3},{4,36},{36... | collective-permute-start | bytes 6291464 | tf_op jit(solution)/shard_map/ppermute | solution.py:33
  158.7 8.7 %collective-permute-start.5 = (bf16[128,1024]{1,0:T(8,128)(2,1)S(1)}, bf16[128,1024]{1,0:T(8,128)(2,1)}, u32[]{:S(2)}, u32[]{:S(2)}) collective-permute-start(bf16[128,1024]{1,0:T(8,128)(2,1)S(1)} %add_convert_fusion.1.refs_0_.a_ref), channel_id=1, source_target_pairs={{0,64},{64,0},{1,65},{65,1},{2,66},{66,2},{3,67},{67,3},{4,68},{68... | collective-permute-start | bytes 786440 | tf_op jit(solution)/shard_map/ppermute | solution.py:33
  160.1 7.3 %copy-start.3 = (bf16[768,1280]{1,0:T(8,128)(2,1)S(1)}, bf16[768,1280]{1,0:T(8,128)(2,1)}, u32[]{:S(2)}) copy-start(bf16[768,1280]{1,0:T(8,128)(2,1)} %all-gather.4.cloned.1.call-done.s_ref.p0.p1) | copy-start | bytes 5898244
  160.1 7.3 %copy-start.5 = (bf16[2,2,256,256]{3,2,1,0:T(8,128)(2,1)S(1)}, bf16[2,2,256,256]{3,2,1,0:T(8,128)(2,1)}, u32[]{:S(2)}) copy-start(bf16[2,2,256,256]{3,2,1,0:T(8,128)(2,1)} %w2.1) | copy-start | bytes 1572868
  167.4 3.6 %copy-start.8 = (bf16[4,8,128,128]{3,2,1,0:T(8,128)(2,1)}, bf16[4,8,128,128]{3,2,1,0:T(8,128)(2,1)S(1)}, u32[]{:S(2)}) copy-start(bf16[4,8,128,128]{3,2,1,0:T(8,128)(2,1)S(1)} %get-tuple-element.26) | copy-start | bytes 3145732
  171.7 3.1 %collective-permute-start.6 = (bf16[128,1536]{1,0:T(8,128)(2,1)}, bf16[128,1536]{1,0:T(8,128)(2,1)S(1)}, u32[]{:S(2)}, u32[]{:S(2)}) collective-permute-start(bf16[128,1536]{1,0:T(8,128)(2,1)} %get-tuple-element.27), channel_id=1, source_target_pairs={{0,32},{32,0},{1,33},{33,1},{2,34},{34,2},{3,35},{35,3},{4,36},{36... | collective-permute-start | bytes 1179656 | tf_op jit(solution)/shard_map/ppermute | solution.py:33
  172.9 25.0 %collective-permute-start.4 = (bf16[4,8,128,128]{3,2,1,0:T(8,128)(2,1)}, bf16[4,8,128,128]{3,2,1,0:T(8,128)(2,1)S(1)}, u32[]{:S(2)}, u32[]{:S(2)}) collective-permute-start(bf16[4,8,128,128]{3,2,1,0:T(8,128)(2,1)} %copy-done.8), channel_id=1, source_target_pairs={{0,64},{64,0},{1,65},{65,1},{2,66},{66,2},{3,67},{67,3},{4,68},{68... | collective-permute-start | bytes 3145736 | tf_op jit(solution)/shard_map/ppermute | solution.py:33
  174.9 12.8 %copy-start.13 = (bf16[128,1536]{1,0:T(8,128)(2,1)}, bf16[128,1536]{1,0:T(8,128)(2,1)S(1)}, u32[]{:S(2)}) copy-start(bf16[128,1536]{1,0:T(8,128)(2,1)S(1)} %broadcast_select_fusion.refs_4_) | copy-start | bytes 1179652
  174.9 11.2 %collective-permute-start.7 = (bf16[128,1536]{1,0:T(8,128)(2,1)S(1)}, bf16[128,1536]{1,0:T(8,128)(2,1)S(1)}, u32[]{:S(2)}, u32[]{:S(2)}) collective-permute-start(bf16[128,1536]{1,0:T(8,128)(2,1)S(1)} %broadcast_select_fusion.refs_4_), channel_id=1, source_target_pairs={{0,1},{1,2},{2,3},{3,0},{4,5},{5,6},{6,7},{7,4},{8,9},{9,10},{10,1... | collective-permute-start | bytes 1179656 | tf_op jit(solution)/shard_map/ppermute | solution.py:29
  177.1 9.0 %collective-permute-start.8 = (bf16[128,1536]{1,0:T(8,128)(2,1)S(1)}, bf16[128,1536]{1,0:T(8,128)(2,1)S(1)}, u32[]{:S(2)}, u32[]{:S(2)}) collective-permute-start(bf16[128,1536]{1,0:T(8,128)(2,1)S(1)} %broadcast_select_fusion.refs_4_), channel_id=1, source_target_pairs={{0,3},{1,0},{2,1},{3,2},{4,7},{5,4},{6,5},{7,6},{8,11},{9,8},{10,9... | collective-permute-start | bytes 1179656 | tf_op jit(solution)/shard_map/ppermute | solution.py:29
  178.3 9.7 %collective-permute-start.10 = (bf16[128,1024]{1,0:T(8,128)(2,1)}, bf16[128,1024]{1,0:T(8,128)(2,1)S(1)}, u32[]{:S(2)}, u32[]{:S(2)}) collective-permute-start(bf16[128,1024]{1,0:T(8,128)(2,1)} %copy-done.6), channel_id=1, source_target_pairs={{0,4},{4,8},{8,12},{12,16},{16,20},{20,24},{24,28},{28,0},{1,5},{5... | collective-permute-start | bytes 786440 | tf_op jit(solution)/shard_map/ppermute | solution.py:29
  179.5 8.5 %collective-permute-start.11 = (bf16[128,1024]{1,0:T(8,128)(2,1)}, bf16[128,1024]{1,0:T(8,128)(2,1)}, u32[]{:S(2)}, u32[]{:S(2)}) collective-permute-start(bf16[128,1024]{1,0:T(8,128)(2,1)} %copy-done.6), channel_id=1, source_target_pairs={{0,28},{4,0},{8,4},{12,8},{16,12},{20,16},{24,20},{28,24},{1,29},{... | collective-permute-start | bytes 786440 | tf_op jit(solution)/shard_map/ppermute | solution.py:29
  187.7 11.6 %collective-permute-start.9 = (bf16[128,1536]{1,0:T(8,128)(2,1)}, bf16[128,1536]{1,0:T(8,128)(2,1)S(1)}, u32[]{:S(2)}, u32[]{:S(2)}) collective-permute-start(bf16[128,1536]{1,0:T(8,128)(2,1)} %get-tuple-element.28.refs_7_), channel_id=1, source_target_pairs={{0,1},{1,2},{2,3},{3,0},{4,5},{5,6},{6,7},{7,4},{8,9},{9,10},{10,1... | collective-permute-start | bytes 1179656 | tf_op jit(solution)/shard_map/ppermute | solution.py:29
  188.7 15.8 %collective-permute-start.12 = (bf16[128,1024]{1,0:T(8,128)(2,1)}, bf16[128,1024]{1,0:T(8,128)(2,1)S(1)}, u32[]{:S(2)}, u32[]{:S(2)}) collective-permute-start(bf16[128,1024]{1,0:T(8,128)(2,1)} %get-tuple-element.32.refs_15_), channel_id=1, source_target_pairs={{0,4},{4,8},{8,12},{12,16},{16,20},{20,24},{24,28},{28,0},{1,5},{5... | collective-permute-start | bytes 786440 | tf_op jit(solution)/shard_map/ppermute | solution.py:29
  189.4 15.0 %collective-permute-start.13 = (bf16[128,1024]{1,0:T(8,128)(2,1)}, bf16[128,1024]{1,0:T(8,128)(2,1)S(1)}, u32[]{:S(2)}, u32[]{:S(2)}) collective-permute-start(bf16[128,1024]{1,0:T(8,128)(2,1)} %get-tuple-element.31.refs_9_), channel_id=1, source_target_pairs={{0,28},{4,0},{8,4},{12,8},{16,12},{20,16},{24,20},{28,24},{1,29},{... | collective-permute-start | bytes 786440 | tf_op jit(solution)/shard_map/ppermute | solution.py:29
  200.1 23.4 %all-to-all-start.2 = ((bf16[4,8,128,128]{3,2,1,0:T(8,128)(2,1)}), bf16[4,8,128,128]{3,2,1,0:T(8,128)(2,1)S(1)}, u32[]{:S(2)}, u32[]{:S(2)}) async-start(bf16[4,8,128,128]{3,2,1,0:T(8,128)(2,1)} %shard_map.63), calls=%async_computation.2 | async-start | bytes 2097152 | tf_op jit(solution)/shard_map/all_to_all | solution.py:451
  205.9 8.8 %collective-permute-start.14 = (bf16[128,1024]{1,0:T(8,128)(2,1)}, bf16[128,1024]{1,0:T(8,128)(2,1)S(1)}, u32[]{:S(2)}, u32[]{:S(2)}) collective-permute-start(bf16[128,1024]{1,0:T(8,128)(2,1)} %get-tuple-element.34.refs_14_), channel_id=1, source_target_pairs={{0,4},{4,8},{8,12},{12,16},{16,20},{20,24},{24,28},{28,0},{1,5},{5... | collective-permute-start | bytes 786440 | tf_op jit(solution)/shard_map/ppermute | solution.py:29
  207.1 8.2 %collective-permute-start.15 = (bf16[128,1024]{1,0:T(8,128)(2,1)}, bf16[128,1024]{1,0:T(8,128)(2,1)S(1)}, u32[]{:S(2)}, u32[]{:S(2)}) collective-permute-start(bf16[128,1024]{1,0:T(8,128)(2,1)} %get-tuple-element.33.refs_10_), channel_id=1, source_target_pairs={{0,28},{4,0},{8,4},{12,8},{16,12},{20,16},{24,20},{28,24},{1,29},{... | collective-permute-start | bytes 786440 | tf_op jit(solution)/shard_map/ppermute | solution.py:29
  216.1 7.4 %collective-permute-start.16 = (bf16[128,1024]{1,0:T(8,128)(2,1)}, bf16[128,1024]{1,0:T(8,128)(2,1)S(1)}, u32[]{:S(2)}, u32[]{:S(2)}) collective-permute-start(bf16[128,1024]{1,0:T(8,128)(2,1)} %get-tuple-element.36.refs_13_), channel_id=1, source_target_pairs={{0,4},{4,8},{8,12},{12,16},{16,20},{20,24},{24,28},{28,0},{1,5},{5... | collective-permute-start | bytes 786440 | tf_op jit(solution)/shard_map/ppermute | solution.py:29
  223.5 1.1 copy-start.9
  224.6 29.2 %copy-start.7 = (s32[2]{0:T(128)S(1)}, s32[2]{0:T(128)}, u32[]{:S(2)}) copy-start(s32[2]{0:T(128)} %pad_add_fusion.zs) | copy-start | bytes 28
  (10 other events, 7.2 us)
Sparse Core Ops, SparseCore 0:
  51.4 96.4 all-gather.3
  175.0 34.6 all-gather.5

commit v3 on v2

--- a/solution.py
+++ b/solution.py
@@ -156,7 +156,7 @@
             out_specs=pl.BlockSpec(shape, lambda g, s: (0, 0, 0)),
         ),
         cost_estimate=cost(1.3),
-        compiler_params=params(),
+        compiler_params=params(LARGE),
     )(source, *[slab] * n)
 
 
@@ -431,9 +431,10 @@
     group = jnp.stack([yp, q])
     lead = lead_rows(special, pivots_one, group)
     keep, send = panel_blocks(rows, panel_src, panel_ok, core, *lead)
-    mine = (keep.astype(F32) + flip(send, "core").astype(F32)).astype(BF)
+    got = flip(send, "core")
+    mine = (keep.astype(F32) + got.astype(F32)).astype(BF)
     other = flip(mine, "yp")
-    tile_got = flip(core_send(rows, source, core, mine), "core")
+    tile_got = flip(tie((core_send(rows, source, core, keep),), got)[0], "core")
     first = jnp.concatenate([
         jnp.where(yp == 0, mine, other)[:, :PANEL], jnp.where(yp == 0, other, mine)[:, :PANEL]], axis=1)
     first = lax.all_gather(first, "z", axis=0, tiled=False)
@@ -447,7 +448,6 @@
     x1 = tie(both_ways((lower, lower), "x", NX))
     parts = (own.astype(F32) + flip(theirs, "yp").astype(F32)).astype(BF)
     x2 = shift(x1[0], "x", 1, NX)
-    parts, = tie((parts,), x2)
     parts = lax.all_to_all(parts, "x", split_axis=0, concat_axis=0, tiled=True)
     z2 = tie(both_ways(z1, "z", NZ))
     z3 = tie(both_ways(z2, "z", NZ))

time: 263 us -> 260 us (0.989)
  waiting for transfers between devices: 136 us -> 131 us
  other arithmetic: 6.03 us -> 8.71 us
    ppermute x7, waiting for transfers between devices: 13.3 us -> 6.34 us  [flip(): return lax.ppermute(v, axis, [(0, 1), (1, 0)])]
    ppermute x10, waiting for transfers between devices: 17.4 us -> 20.4 us  [shift(): return lax.ppermute(v, axis, [(i, (i + step) % n) for i in range(n)])]
    unnamed x40 -> x38, local copies, waits for them, and re-layouts: 10.7 us -> 9.34 us
  transfers between devices with their start and end apart: 22 -> 22, of which waited for: 11 -> 11; matrix products, arithmetic and copies ran while one was open for 4% -> 5% of each run, Pallas kernels for 3% -> 5%
where the time goes in v3:
time: 260 us; the launch traced here: 259 us
  waiting for transfers between devices  131 us (50%)
  starting transfers between devices  42.9 us (16%)
  Pallas kernels  26.4 us (10%)
  blocking collectives  20.2 us (8%)
  local copies, waits for them, and re-layouts  15.7 us (6%)
  between operations  13.7 us (5%)
  other arithmetic  8.71 us (3%)
    all_gather x1, waiting for transfers between devices, local(): special = lax.all_gather(special, ('z', 'x'), axis=0, tiled=True)  95.6 us
    ppermute x10, waiting for transfers between devices, shift(): return lax.ppermute(v, axis, [(i, (i + step) % n) for i in range(n)])  20.4 us
    all_to_all x1, blocking collectives, local(): lax.all_to_all(done, ('core', 'x'), split_axis=0, concat_axis=0, tiled=True)  20.2 us
    ppermute x10, starting transfers between devices, shift(): return lax.ppermute(v, axis, [(i, (i + step) % n) for i in range(n)])  13.2 us
    all_to_all x1, starting transfers between devices, local(): lax.all_to_all(first, ('z', 'x'), split_axis=0, concat_axis=0, tiled=True)  11.9 us
    unnamed x38, local copies, waits for them, and re-layouts  9.34 us
    all_to_all x1, waiting for transfers between devices, local(): lax.all_to_all(first, ('z', 'x'), split_axis=0, concat_axis=0, tiled=True)  8.75 us
    ppermute x7, starting transfers between devices, flip(): return lax.ppermute(v, axis, [(0, 1), (1, 0)])  8.15 us
  transfers between devices with their start and end apart: 22, of which 11 were waited for; matrix products, arithmetic and copies ran while one was open for 5% of the time, Pallas kernels for 5%

profile of v3, /device:TPU:1, one launch (start us, length us, event | category | flops | bytes accessed | tf_op | source)
XLA Modules:
  0.0 258.8 jit_solution(15366854328912425458)
XLA Ops:
  8.8 2.4 shard_map.55
  11.2 11.9 %all-to-all-start.1 = ((bf16[32,24,256]{2,1,0:T(8,128)(2,1)}), bf16[32,24,256]{2,1,0:T(8,128)(2,1)S(1)}, u32[]{:S(2)}, u32[]{:S(2)}) async-start(bf16[32,24,256]{2,1,0:T(8,128)(2,1)} %bitcast.31), calls=%async_computation.1 | async-start | bytes 786432 | tf_op jit(solution)/shard_map/all_to_all | solution.py:411
  23.1 5.0 %gather_fusion = bf16[64,128,256]{2,1,0:T(8,128)(2,1)} fusion(bf16[64,128,256]{2,1,0:T(8,128)(2,1)} %bitcast.27, s32[1024]{0:T(1024)S(1)} %pad_clamp_fusion), kind=kCustom, calls=%fused_computation | custom fusion | bytes 8388864 | tf_op jit(solution)/shard_map/gather | solution.py:425
  28.2 8.7 %all-to-all-done.1.refs_0_.refs_1_.refs_2_.refs_3_.refs_4_.refs_5_ = bf16[32,24,256]{2,1,0:T(8,128)(2,1)S(1)} async-done(((bf16[32,24,256]{2,1,0:T(8,128)(2,1)}), bf16[32,24,256]{2,1,0:T(8,128)(2,1)S(1)}, u32[]{:S(2)}, u32[]{:S(2)}) %all-to-all-start.1) | async-done | bytes 393248 | tf_op jit(solution)/shard_map/all_to_all | solution.py:411
  36.9 5.3 %all-to-all-start = ((bf16[32,256,256]{2,1,0:T(8,128)(2,1)}), bf16[32,256,256]{2,1,0:T(8,128)(2,1)}, u32[]{:S(2)}, u32[]{:S(2)}) async-start(bf16[32,256,256]{2,1,0:T(8,128)(2,1)} %bitcast.28), calls=%async_computation | async-start | bytes 8388608 | tf_op jit(solution)/shard_map/all_to_all | solution.py:426
  43.4 2.3 collective-permute-start
  46.7 1.4 collective-permute-start.1
  48.1 1.9 collective-permute-done.1
  51.1 95.6 %all-gather.4.cloned.1.call-done.s_ref.p0.p1 = bf16[768,1280]{1,0:T(8,128)(2,1)} async-done(((bf16[24,1280]{1,0:T(8,128)(2,1)}), bf16[768,1280]{1,0:T(8,128)(2,1)}) %all-gather.4.cloned.1.call-update) | async-done | bytes 1966096 | tf_op jit(solution)/shard_map/all_gather | solution.py:423
  146.7 1.5 copy-done.1
  148.3 1.6 shard_map.57
  149.9 1.8 shard_map.58
  152.9 2.5 shard_map.59.refs_0_
  155.4 1.4 copy-done.3
  158.6 1.4 collective-permute-start.5
  160.3 1.7 collective-permute-done.3.refs_8_
  162.0 5.0 %shard_map.61 = (bf16[4,8,128,128]{3,2,1,0:T(8,128)(2,1)S(1)}, bf16[4,8,128,128]{3,2,1,0:T(8,128)(2,1)}) custom-call(s32[64]{0:T(128)S(1)} %select_reduce_fusion.src, s32[128]{0:T(128)S(1)} %mul.71.okr, s32[2]{0:T(128)S(1)} %pad_add_fusion.1.ce, bf16[32,256,256]{2,1,0:T(8,128)(2,1)} %all-to-all-done.refs_0_.refs_1_.refs_2_.refs_3_.refs_4_.refs_5_.refs_6_.refs_7_.rows_ref, ...), custom_call_target="tpu_custom_call" | custom-call | bytes 1512000 | tf_op jit(solution)/shard_map/pallas_call | solution.py:210
  168.4 3.6 %shard_map.62 = (bf16[128,1024]{1,0:T(8,128)(2,1)}, bf16[128,1536]{1,0:T(8,128)(2,1)}) custom-call(s32[2]{0:T(128)S(1)} %pad_add_fusion.3.y, bf16[128,1024]{1,0:T(8,128)(2,1)S(1)} %add_convert_fusion.1.a_ref, bf16[128,1024]{1,0:T(8,128)(2,1)} %collective-permute-done.5.b_ref, bf16[768,1280]{1,0:T(8,128)(2,1)S(1)} %copy-done.2, ...), custom_call_target="tpu_custom_call" | custom-call | bytes 1260000 | tf_op jit(solution)/shard_map/pallas_call | solution.py:298
  173.3 1.8 collective-permute-start.10
  176.8 5.9 %collective-permute-done.10.refs_0_ = bf16[128,1024]{1,0:T(8,128)(2,1)S(1)} collective-permute-done((bf16[128,1024]{1,0:T(8,128)(2,1)}, bf16[128,1024]{1,0:T(8,128)(2,1)S(1)}, u32[]{:S(2)}, u32[]{:S(2)}) %collective-permute-start.10) | collective-permute-done | bytes 262176 | tf_op jit(solution)/shard_map/ppermute | solution.py:29
  185.1 1.6 collective-permute-start.13
  186.9 2.2 collective-permute-start.7
  190.2 1.8 collective-permute-done.4
  192.0 2.5 add_convert_fusion
  194.5 4.4 %all-to-all-start.2 = ((bf16[4,8,128,128]{3,2,1,0:T(8,128)(2,1)}), bf16[4,8,128,128]{3,2,1,0:T(8,128)(2,1)S(1)}, u32[]{:S(2)}, u32[]{:S(2)}) async-start(bf16[4,8,128,128]{3,2,1,0:T(8,128)(2,1)} %add_convert_fusion), calls=%async_computation.2 | async-start | bytes 2097152 | tf_op jit(solution)/shard_map/all_to_all | solution.py:451
  200.5 1.8 collective-permute-start.15
  203.8 1.8 collective-permute-start.9
  205.6 6.2 %collective-permute-done.14.refs_0_ = bf16[128,1024]{1,0:T(8,128)(2,1)S(1)} collective-permute-done((bf16[128,1024]{1,0:T(8,128)(2,1)}, bf16[128,1024]{1,0:T(8,128)(2,1)S(1)}, u32[]{:S(2)}, u32[]{:S(2)}) %collective-permute-start.14) | collective-permute-done | bytes 262176 | tf_op jit(solution)/shard_map/ppermute | solution.py:29
  213.8 6.9 %collective-permute-done.16.refs_12_ = bf16[128,1024]{1,0:T(8,128)(2,1)S(1)} collective-permute-done((bf16[128,1024]{1,0:T(8,128)(2,1)}, bf16[128,1024]{1,0:T(8,128)(2,1)S(1)}, u32[]{:S(2)}, u32[]{:S(2)}) %collective-permute-start.16) | collective-permute-done | bytes 262176 | tf_op jit(solution)/shard_map/ppermute | solution.py:29
  222.8 7.1 %shard_map.67 = bf16[8,8,64,128]{3,2,1,0:T(8,128)(2,1)} custom-call(s32[2]{0:T(128)} %pad_add_fusion.zs, bf16[4,8,128,128]{3,2,1,0:T(8,128)(2,1)} %copy-done.7, bf16[4,8,128,128]{3,2,1,0:T(8,128)(2,1)} %copy-done.7, bf16[8,128,512]{2,1,0:T(8,128)(2,1)} %bitcast.29, bf16[8,128,512]{2,1,0:T(8,128)(2,1)} %bitcast.30, bf16[128,1536]{1,0:T(8,128)(2,1)} %copy-done.10, ...), custom_call_target="tpu_custom_call" | custom-call | bytes 2520000 | tf_op jit(solution)/shard_map/pallas_call | solution.py:352
  229.8 20.2 %all_to_all.20.refs_0_.refs_1_.refs_2_.refs_3_ = bf16[8,8,64,128]{3,2,1,0:T(8,128)(2,1)S(1)} all-to-all(bf16[8,8,64,128]{3,2,1,0:T(8,128)(2,1)} %shard_map.67), channel_id=1, replica_groups=mesh['q'=2,'yp'=2,'core'=2,'z'=8,'x'=4] {'core','x'}, dimensions={0} | all-to-all | bytes 2097152 | tf_op jit(solution)/shard_map/all_to_all | solution.py:459
  250.1 1.8 shard_map.68
  (112 shorter events, 23.9 us)
Async XLA Ops:
  6.5 1.3 copy-start
  11.2 25.7 %all-to-all-start.1 = ((bf16[32,24,256]{2,1,0:T(8,128)(2,1)}), bf16[32,24,256]{2,1,0:T(8,128)(2,1)S(1)}, u32[]{:S(2)}, u32[]{:S(2)}) async-start(bf16[32,24,256]{2,1,0:T(8,128)(2,1)} %bitcast.31), calls=%async_computation.1 | async-start | bytes 786432 | tf_op jit(solution)/shard_map/all_to_all | solution.py:411
  36.9 109.8 %copy-start.4 = (bf16[4,2,256,256]{3,2,1,0:T(8,128)(2,1)S(1)}, bf16[4,2,256,256]{3,2,1,0:T(8,128)(2,1)}, u32[]{:S(2)}) copy-start(bf16[4,2,256,256]{3,2,1,0:T(8,128)(2,1)} %w1.3) | copy-start | bytes 3145732
  36.9 113.0 %all-to-all-start = ((bf16[32,256,256]{2,1,0:T(8,128)(2,1)}), bf16[32,256,256]{2,1,0:T(8,128)(2,1)}, u32[]{:S(2)}, u32[]{:S(2)}) async-start(bf16[32,256,256]{2,1,0:T(8,128)(2,1)} %bitcast.28), calls=%async_computation | async-start | bytes 8388608 | tf_op jit(solution)/shard_map/all_to_all | solution.py:426
  42.2 104.6 %all-gather.4.cloned.1.call-start = ((), (), s32[]{:S(2)}) async-start(), calls=%async_computation.4 | async-start | bytes 2027520 | tf_op jit(solution)/shard_map/all_gather | solution.py:423
  43.4 3.2 %collective-permute-start = (bf16[24,768]{1,0:T(8,128)(2,1)S(1)}, bf16[24,768]{1,0:T(8,128)(2,1)S(1)}, u32[]{:S(2)}, u32[]{:S(2)}) collective-permute-start(bf16[24,768]{1,0:T(8,128)(2,1)S(1)} %fusion), channel_id=1, source_target_pairs={{0,32},{32,0},{1,33},{33,1},{2,34},{34,2},{3,35},{35,3},{4,36},{36... | collective-permute-start | bytes 110600 | tf_op jit(solution)/shard_map/ppermute | solution.py:33
  46.7 3.3 %collective-permute-start.1 = (bf16[24,768]{1,0:T(8,128)(2,1)S(1)}, bf16[24,768]{1,0:T(8,128)(2,1)S(1)}, u32[]{:S(2)}, u32[]{:S(2)}) collective-permute-start(bf16[24,768]{1,0:T(8,128)(2,1)S(1)} %add_convert_fusion.2), channel_id=1, source_target_pairs={{0,64},{64,0},{1,65},{65,1},{2,66},{66,2},{3,67},{67,3},{4,68},{68... | collective-permute-start | bytes 110600 | tf_op jit(solution)/shard_map/ppermute | solution.py:33
  50.7 163.1 %all-gather.6.cloned.1.call-start = ((), (), s32[]{:S(2)}) async-start(), calls=%async_computation.5 | async-start | bytes 1179648 | tf_op jit(solution)/shard_map/all_gather | solution.py:440
  146.7 1.5 copy-start.1
  151.7 5.2 %collective-permute-start.2 = (bf16[128,1024]{1,0:T(8,128)(2,1)S(1)}, bf16[128,1024]{1,0:T(8,128)(2,1)S(1)}, u32[]{:S(2)}, u32[]{:S(2)}) collective-permute-start(bf16[128,1024]{1,0:T(8,128)(2,1)S(1)} %get-tuple-element.24), channel_id=1, source_target_pairs={{0,32},{32,0},{1,33},{33,1},{2,34},{34,2},{3,35},{35,3},{4,36},{36... | collective-permute-start | bytes 786440 | tf_op jit(solution)/shard_map/ppermute | solution.py:33
  155.4 1.4 copy-start.3
  157.5 4.5 %collective-permute-start.3 = (bf16[4,8,256,128]{3,2,1,0:T(8,128)(2,1)}, bf16[4,8,256,128]{3,2,1,0:T(8,128)(2,1)}, u32[]{:S(2)}, u32[]{:S(2)}) collective-permute-start(bf16[4,8,256,128]{3,2,1,0:T(8,128)(2,1)} %shard_map.60), channel_id=1, source_target_pairs={{0,32},{32,0},{1,33},{33,1},{2,34},{34,2},{3,35},{35,3},{4,36},{36... | collective-permute-start | bytes 6291464 | tf_op jit(solution)/shard_map/ppermute | solution.py:33
  158.6 9.8 %collective-permute-start.5 = (bf16[128,1024]{1,0:T(8,128)(2,1)S(1)}, bf16[128,1024]{1,0:T(8,128)(2,1)}, u32[]{:S(2)}, u32[]{:S(2)}) collective-permute-start(bf16[128,1024]{1,0:T(8,128)(2,1)S(1)} %add_convert_fusion.1.a_ref), channel_id=1, source_target_pairs={{0,64},{64,0},{1,65},{65,1},{2,66},{66,2},{3,67},{67,3},{4,68},{68... | collective-permute-start | bytes 786440 | tf_op jit(solution)/shard_map/ppermute | solution.py:33
  160.3 8.1 %copy-start.2 = (bf16[768,1280]{1,0:T(8,128)(2,1)S(1)}, bf16[768,1280]{1,0:T(8,128)(2,1)}, u32[]{:S(2)}) copy-start(bf16[768,1280]{1,0:T(8,128)(2,1)} %all-gather.4.cloned.1.call-done.s_ref.p0.p1) | copy-start | bytes 5898244
  160.3 8.1 %copy-start.5 = (bf16[2,2,256,256]{3,2,1,0:T(8,128)(2,1)S(1)}, bf16[2,2,256,256]{3,2,1,0:T(8,128)(2,1)}, u32[]{:S(2)}) copy-start(bf16[2,2,256,256]{3,2,1,0:T(8,128)(2,1)} %w2.1) | copy-start | bytes 1572868
  167.1 24.9 %collective-permute-start.4 = (bf16[4,8,128,128]{3,2,1,0:T(8,128)(2,1)}, bf16[4,8,128,128]{3,2,1,0:T(8,128)(2,1)}, u32[]{:S(2)}, u32[]{:S(2)}) collective-permute-start(bf16[4,8,128,128]{3,2,1,0:T(8,128)(2,1)} %get-tuple-element.26), channel_id=1, source_target_pairs={{0,64},{64,0},{1,65},{65,1},{2,66},{66,2},{3,67},{67,3},{4,68},{68... | collective-permute-start | bytes 3145736 | tf_op jit(solution)/shard_map/ppermute | solution.py:33
  172.0 14.8 %collective-permute-start.6 = (bf16[128,1536]{1,0:T(8,128)(2,1)}, bf16[128,1536]{1,0:T(8,128)(2,1)S(1)}, u32[]{:S(2)}, u32[]{:S(2)}) collective-permute-start(bf16[128,1536]{1,0:T(8,128)(2,1)} %get-tuple-element.27), channel_id=1, source_target_pairs={{0,32},{32,0},{1,33},{33,1},{2,34},{34,2},{3,35},{35,3},{4,36},{36... | collective-permute-start | bytes 1179656 | tf_op jit(solution)/shard_map/ppermute | solution.py:33
  173.3 9.4 %collective-permute-start.10 = (bf16[128,1024]{1,0:T(8,128)(2,1)}, bf16[128,1024]{1,0:T(8,128)(2,1)S(1)}, u32[]{:S(2)}, u32[]{:S(2)}) collective-permute-start(bf16[128,1024]{1,0:T(8,128)(2,1)} %get-tuple-element.30.refs_8_), channel_id=1, source_target_pairs={{0,4},{4,8},{8,12},{12,16},{16,20},{20,24},{24,28},{28,0},{1,5},{5... | collective-permute-start | bytes 786440 | tf_op jit(solution)/shard_map/ppermute | solution.py:29
  175.1 8.1 %collective-permute-start.11 = (bf16[128,1024]{1,0:T(8,128)(2,1)}, bf16[128,1024]{1,0:T(8,128)(2,1)S(1)}, u32[]{:S(2)}, u32[]{:S(2)}) collective-permute-start(bf16[128,1024]{1,0:T(8,128)(2,1)} %get-tuple-element.30.refs_8_), channel_id=1, source_target_pairs={{0,28},{4,0},{8,4},{12,8},{16,12},{20,16},{24,20},{28,24},{1,29},{... | collective-permute-start | bytes 786440 | tf_op jit(solution)/shard_map/ppermute | solution.py:29
  184.1 14.8 %collective-permute-start.12 = (bf16[128,1024]{1,0:T(8,128)(2,1)}, bf16[128,1024]{1,0:T(8,128)(2,1)S(1)}, u32[]{:S(2)}, u32[]{:S(2)}) collective-permute-start(bf16[128,1024]{1,0:T(8,128)(2,1)} %get-tuple-element.32.refs_15_), channel_id=1, source_target_pairs={{0,4},{4,8},{8,12},{12,16},{16,20},{20,24},{24,28},{28,0},{1,5},{5... | collective-permute-start | bytes 786440 | tf_op jit(solution)/shard_map/ppermute | solution.py:29
  185.1 13.8 %collective-permute-start.13 = (bf16[128,1024]{1,0:T(8,128)(2,1)}, bf16[128,1024]{1,0:T(8,128)(2,1)}, u32[]{:S(2)}, u32[]{:S(2)}) collective-permute-start(bf16[128,1024]{1,0:T(8,128)(2,1)} %get-tuple-element.31.refs_9_), channel_id=1, source_target_pairs={{0,28},{4,0},{8,4},{12,8},{16,12},{20,16},{24,20},{28,24},{1,29},{... | collective-permute-start | bytes 786440 | tf_op jit(solution)/shard_map/ppermute | solution.py:29
  186.8 34.8 %copy-start.10 = (bf16[128,1536]{1,0:T(8,128)(2,1)}, bf16[128,1536]{1,0:T(8,128)(2,1)S(1)}, u32[]{:S(2)}) copy-start(bf16[128,1536]{1,0:T(8,128)(2,1)S(1)} %broadcast_select_fusion.refs_4_) | copy-start | bytes 1179652
  186.9 15.4 %collective-permute-start.7 = (bf16[128,1536]{1,0:T(8,128)(2,1)S(1)}, bf16[128,1536]{1,0:T(8,128)(2,1)S(1)}, u32[]{:S(2)}, u32[]{:S(2)}) collective-permute-start(bf16[128,1536]{1,0:T(8,128)(2,1)S(1)} %broadcast_select_fusion.refs_4_), channel_id=1, source_target_pairs={{0,1},{1,2},{2,3},{3,0},{4,5},{5,6},{6,7},{7,4},{8,9},{9,10},{10,1... | collective-permute-start | bytes 1179656 | tf_op jit(solution)/shard_map/ppermute | solution.py:29
  189.1 13.2 %collective-permute-start.8 = (bf16[128,1536]{1,0:T(8,128)(2,1)S(1)}, bf16[128,1536]{1,0:T(8,128)(2,1)S(1)}, u32[]{:S(2)}, u32[]{:S(2)}) collective-permute-start(bf16[128,1536]{1,0:T(8,128)(2,1)S(1)} %broadcast_select_fusion.refs_4_), channel_id=1, source_target_pairs={{0,3},{1,0},{2,1},{3,2},{4,7},{5,4},{6,5},{7,6},{8,11},{9,8},{10,9... | collective-permute-start | bytes 1179656 | tf_op jit(solution)/shard_map/ppermute | solution.py:29
  194.5 27.2 %all-to-all-start.2 = ((bf16[4,8,128,128]{3,2,1,0:T(8,128)(2,1)}), bf16[4,8,128,128]{3,2,1,0:T(8,128)(2,1)S(1)}, u32[]{:S(2)}, u32[]{:S(2)}) async-start(bf16[4,8,128,128]{3,2,1,0:T(8,128)(2,1)} %add_convert_fusion), calls=%async_computation.2 | async-start | bytes 2097152 | tf_op jit(solution)/shard_map/all_to_all | solution.py:451
  199.6 12.1 %collective-permute-start.14 = (bf16[128,1024]{1,0:T(8,128)(2,1)}, bf16[128,1024]{1,0:T(8,128)(2,1)S(1)}, u32[]{:S(2)}, u32[]{:S(2)}) collective-permute-start(bf16[128,1024]{1,0:T(8,128)(2,1)} %get-tuple-element.34.refs_14_), channel_id=1, source_target_pairs={{0,4},{4,8},{8,12},{12,16},{16,20},{20,24},{24,28},{28,0},{1,5},{5... | collective-permute-start | bytes 786440 | tf_op jit(solution)/shard_map/ppermute | solution.py:29
  200.5 11.3 %collective-permute-start.15 = (bf16[128,1024]{1,0:T(8,128)(2,1)}, bf16[128,1024]{1,0:T(8,128)(2,1)S(1)}, u32[]{:S(2)}, u32[]{:S(2)}) collective-permute-start(bf16[128,1024]{1,0:T(8,128)(2,1)} %get-tuple-element.33.refs_10_), channel_id=1, source_target_pairs={{0,28},{4,0},{8,4},{12,8},{16,12},{20,16},{24,20},{28,24},{1,29},{... | collective-permute-start | bytes 786440 | tf_op jit(solution)/shard_map/ppermute | solution.py:29
  203.8 17.9 %collective-permute-start.9 = (bf16[128,1536]{1,0:T(8,128)(2,1)}, bf16[128,1536]{1,0:T(8,128)(2,1)S(1)}, u32[]{:S(2)}, u32[]{:S(2)}) collective-permute-start(bf16[128,1536]{1,0:T(8,128)(2,1)} %get-tuple-element.29.refs_7_), channel_id=1, source_target_pairs={{0,1},{1,2},{2,3},{3,0},{4,5},{5,6},{6,7},{7,4},{8,9},{9,10},{10,1... | collective-permute-start | bytes 1179656 | tf_op jit(solution)/shard_map/ppermute | solution.py:29
  213.2 7.6 %collective-permute-start.16 = (bf16[128,1024]{1,0:T(8,128)(2,1)}, bf16[128,1024]{1,0:T(8,128)(2,1)S(1)}, u32[]{:S(2)}, u32[]{:S(2)}) collective-permute-start(bf16[128,1024]{1,0:T(8,128)(2,1)} %get-tuple-element.36.refs_13_), channel_id=1, source_target_pairs={{0,4},{4,8},{8,12},{12,16},{16,20},{20,24},{24,28},{28,0},{1,5},{5... | collective-permute-start | bytes 786440 | tf_op jit(solution)/shard_map/ppermute | solution.py:29
  220.7 0.9 copy-start.18
  221.7 1.1 copy-start.7
  222.8 27.3 %copy-start.6 = (s32[2]{0:T(128)S(1)}, s32[2]{0:T(128)}, u32[]{:S(2)}) copy-start(s32[2]{0:T(128)} %pad_add_fusion.zs) | copy-start | bytes 28
  (9 other events, 6.5 us)
Sparse Core Ops, SparseCore 0:
  50.8 95.8 all-gather.3
  176.9 35.3 all-gather.5

commit v4 on v3

--- a/solution.py
+++ b/solution.py
@@ -268,7 +268,7 @@
     n = PANEL
 
     def body(y, a_ref, b_ref, p0, p1, t_ref, lead_ref, w1, w2, *refs):
-        c_out, l_out = refs[-2:]
+        c_out, l_out, first_out = refs[-3:]
         first = y[0] == 0
         a, b = a_ref[...], b_ref[...]
         both = (jnp.where(first, a, b), jnp.where(first, b, a))
@@ -281,6 +281,7 @@
             c1 = (both[p][:, n:2 * n].astype(F32) - mm_t(l0, (p0, p1)[p][...])).astype(BF)
             l1 = mm(c1, w1[p, 1]).astype(BF)
             panel = panel - mm_t(l0, t_ref[:, low]) - mm_t(l1, t_ref[:, high])
+            first_out[:, p * n:(p + 1) * n] = c0
             c_out[:, p * n:(p + 1) * n] = c1
             l_out[:, p * n:(p + 1) * n] = l0
             l_out[:, (2 + p) * n:(3 + p) * n] = l1
@@ -294,7 +295,7 @@
 
     def whole(v):
         return pl.BlockSpec(v.shape, lambda g, y: (0, 0))
-    out = [jax.ShapeDtypeStruct((BLOCK, k * n), BF) for k in (4, 6)]
+    out = [jax.ShapeDtypeStruct((BLOCK, k * n), BF) for k in (4, 6, 2)]
     return pl.pallas_call(
         body,
         out_shape=out,
@@ -435,11 +436,10 @@
     mine = (keep.astype(F32) + got.astype(F32)).astype(BF)
     other = flip(mine, "yp")
     tile_got = flip(tie((core_send(rows, source, core, keep),), got)[0], "core")
-    first = jnp.concatenate([
-        jnp.where(yp == 0, mine, other)[:, :PANEL], jnp.where(yp == 0, other, mine)[:, :PANEL]], axis=1)
+    own, theirs = core_sum(rows, tile_got, source, tile_ok, jnp.stack([e, yp]))
+    columns, lower, first = factor_rows(mine, other, special, lead, pivots_one, pivots_two, group, own)
+
     first = lax.all_gather(first, "z", axis=0, tiled=False)
-    own, theirs = core_sum(rows, tile_got, source, tile_ok, jnp.stack([e, yp]))
-    columns, lower = factor_rows(mine, other, special, lead, pivots_one, pivots_two, group, own)
 
     place = jnp.stack([z, x])
     z1 = tie(both_ways((columns, columns), "z", NZ))

time: 260 us -> 259 us (level)
    unnamed x38 -> x40, local copies, waits for them, and re-layouts: 9.34 us -> 9.31 us
  transfers between devices with their start and end apart: 22 -> 22, of which waited for: 11 -> 11; matrix products, arithmetic and copies ran while one was open for 5% -> 4% of each run, Pallas kernels for 5% -> 5%
where the time goes in v4:
time: 259 us; the launch traced here: 258 us
  waiting for transfers between devices  132 us (51%)
  starting transfers between devices  43.9 us (17%)
  Pallas kernels  25.5 us (10%)
  blocking collectives  20.2 us (8%)
  local copies, waits for them, and re-layouts  15.6 us (6%)
  between operations  13.7 us (5%)
  other arithmetic  7.21 us (3%)
    all_gather x1, waiting for transfers between devices, local(): special = lax.all_gather(special, ('z', 'x'), axis=0, tiled=True)  95.6 us
    all_to_all x1, blocking collectives, local(): lax.all_to_all(done, ('core', 'x'), split_axis=0, concat_axis=0, tiled=True)  20.2 us
    ppermute x10, waiting for transfers between devices, shift(): return lax.ppermute(v, axis, [(i, (i + step) % n) for i in range(n)])  20 us
    ppermute x10, starting transfers between devices, shift(): return lax.ppermute(v, axis, [(i, (i + step) % n) for i in range(n)])  14.2 us
    all_to_all x1, starting transfers between devices, local(): lax.all_to_all(first, ('z', 'x'), split_axis=0, concat_axis=0, tiled=True)  11.9 us
    unnamed x40, local copies, waits for them, and re-layouts  9.31 us
    all_to_all x1, waiting for transfers between devices, local(): lax.all_to_all(first, ('z', 'x'), split_axis=0, concat_axis=0, tiled=True)  8.75 us
    ppermute x7, starting transfers between devices, flip(): return lax.ppermute(v, axis, [(0, 1), (1, 0)])  8.15 us
  transfers between devices with their start and end apart: 22, of which 11 were waited for; matrix products, arithmetic and copies ran while one was open for 4% of the time, Pallas kernels for 5%

profile of v4, /device:TPU:1, one launch (start us, length us, event | category | flops | bytes accessed | tf_op | source)
XLA Modules:
  0.0 258.4 jit_solution(10496920622122109100)
XLA Ops:
  8.8 2.4 shard_map.55
  11.3 11.9 %all-to-all-start.1 = ((bf16[32,24,256]{2,1,0:T(8,128)(2,1)}), bf16[32,24,256]{2,1,0:T(8,128)(2,1)S(1)}, u32[]{:S(2)}, u32[]{:S(2)}) async-start(bf16[32,24,256]{2,1,0:T(8,128)(2,1)} %bitcast.31), calls=%async_computation.1 | async-start | bytes 786432 | tf_op jit(solution)/shard_map/all_to_all | solution.py:412
  23.2 5.0 %gather_fusion = bf16[64,128,256]{2,1,0:T(8,128)(2,1)} fusion(bf16[64,128,256]{2,1,0:T(8,128)(2,1)} %bitcast.27, s32[1024]{0:T(1024)S(1)} %pad_clamp_fusion), kind=kCustom, calls=%fused_computation | custom fusion | bytes 8388864 | tf_op jit(solution)/shard_map/gather | solution.py:426
  28.2 8.7 %all-to-all-done.1.refs_0_.refs_1_.refs_2_.refs_3_.refs_4_.refs_5_ = bf16[32,24,256]{2,1,0:T(8,128)(2,1)S(1)} async-done(((bf16[32,24,256]{2,1,0:T(8,128)(2,1)}), bf16[32,24,256]{2,1,0:T(8,128)(2,1)S(1)}, u32[]{:S(2)}, u32[]{:S(2)}) %all-to-all-start.1) | async-done | bytes 393248 | tf_op jit(solution)/shard_map/all_to_all | solution.py:412
  37.0 5.3 %all-to-all-start = ((bf16[32,256,256]{2,1,0:T(8,128)(2,1)}), bf16[32,256,256]{2,1,0:T(8,128)(2,1)}, u32[]{:S(2)}, u32[]{:S(2)}) async-start(bf16[32,256,256]{2,1,0:T(8,128)(2,1)} %bitcast.28), calls=%async_computation | async-start | bytes 8388608 | tf_op jit(solution)/shard_map/all_to_all | solution.py:427
  43.5 2.3 collective-permute-start
  48.1 1.9 collective-permute-done.1
  51.2 95.6 %all-gather.4.cloned.1.call-done.s_ref.p0.p1 = bf16[768,1280]{1,0:T(8,128)(2,1)} async-done(((bf16[24,1280]{1,0:T(8,128)(2,1)}), bf16[768,1280]{1,0:T(8,128)(2,1)}) %all-gather.4.cloned.1.call-update) | async-done | bytes 1966096 | tf_op jit(solution)/shard_map/all_gather | solution.py:424
  146.8 1.5 copy-done.1
  148.3 1.6 shard_map.57
  149.9 1.8 shard_map.58
  152.9 2.5 shard_map.59.refs_0_
  155.5 1.4 copy-done.3
  158.8 1.4 collective-permute-start.5
  160.3 1.7 collective-permute-done.3.refs_8_
  162.1 5.0 %shard_map.61 = (bf16[4,8,128,128]{3,2,1,0:T(8,128)(2,1)S(1)}, bf16[4,8,128,128]{3,2,1,0:T(8,128)(2,1)}) custom-call(s32[64]{0:T(128)S(1)} %select_reduce_fusion.src, s32[128]{0:T(128)S(1)} %mul.71.okr, s32[2]{0:T(128)S(1)} %pad_add_fusion.1.ce, bf16[32,256,256]{2,1,0:T(8,128)(2,1)} %all-to-all-done.refs_0_.refs_1_.refs_2_.refs_3_.refs_4_.refs_5_.refs_6_.refs_7_.rows_ref, ...), custom_call_target="tpu_custom_call" | custom-call | bytes 1512000 | tf_op jit(solution)/shard_map/pallas_call | solution.py:210
  168.4 2.7 %shard_map.62 = (bf16[128,1024]{1,0:T(8,128)(2,1)S(1)}, bf16[128,1536]{1,0:T(8,128)(2,1)}, bf16[128,512]{1,0:T(8,128)(2,1)S(1)}) custom-call(s32[2]{0:T(128)S(1)} %pad_add_fusion.3.y, bf16[128,1024]{1,0:T(8,128)(2,1)S(1)} %add_convert_fusion.1.a_ref, bf16[128,1024]{1,0:T(8,128)(2,1)S(1)} %collective-permute-done.5.b_ref, bf16[768,1280]{1,0:T(8,128)(2,1)S(1)} %copy-done.2, ...), custom_call_target="tpu_custom_call" | custom-call | bytes 1260000 | tf_op jit(solution)/shard_map/pallas_call | solution.py:299
  172.2 1.7 collective-permute-start.10
  174.9 6.4 %collective-permute-done.10.refs_0_ = bf16[128,1024]{1,0:T(8,128)(2,1)S(1)} collective-permute-done((bf16[128,1024]{1,0:T(8,128)(2,1)S(1)}, bf16[128,1024]{1,0:T(8,128)(2,1)S(1)}, u32[]{:S(2)}, u32[]{:S(2)}) %collective-permute-start.10) | collective-permute-done | bytes 262176 | tf_op jit(solution)/shard_map/ppermute | solution.py:29
  183.8 1.6 collective-permute-start.13
  185.5 2.2 collective-permute-start.7
  188.7 3.3 %collective-permute-done.4 = bf16[4,8,128,128]{3,2,1,0:T(8,128)(2,1)} collective-permute-done((bf16[4,8,128,128]{3,2,1,0:T(8,128)(2,1)}, bf16[4,8,128,128]{3,2,1,0:T(8,128)(2,1)}, u32[]{:S(2)}, u32[]{:S(2)}) %collective-permute-start.4) | collective-permute-done | bytes 1048608 | tf_op jit(solution)/shard_map/ppermute | solution.py:33
  192.0 2.5 add_convert_fusion
  194.5 4.4 %all-to-all-start.2 = ((bf16[4,8,128,128]{3,2,1,0:T(8,128)(2,1)}), bf16[4,8,128,128]{3,2,1,0:T(8,128)(2,1)S(1)}, u32[]{:S(2)}, u32[]{:S(2)}) async-start(bf16[4,8,128,128]{3,2,1,0:T(8,128)(2,1)} %add_convert_fusion), calls=%async_computation.2 | async-start | bytes 2097152 | tf_op jit(solution)/shard_map/all_to_all | solution.py:451
  199.9 1.8 collective-permute-start.15
  203.2 1.8 collective-permute-start.9
  205.0 5.2 %collective-permute-done.14.refs_0_ = bf16[128,1024]{1,0:T(8,128)(2,1)S(1)} collective-permute-done((bf16[128,1024]{1,0:T(8,128)(2,1)}, bf16[128,1024]{1,0:T(8,128)(2,1)S(1)}, u32[]{:S(2)}, u32[]{:S(2)}) %collective-permute-start.14) | collective-permute-done | bytes 262176 | tf_op jit(solution)/shard_map/ppermute | solution.py:29
  213.3 5.6 %collective-permute-done.16.refs_12_ = bf16[128,1024]{1,0:T(8,128)(2,1)S(1)} collective-permute-done((bf16[128,1024]{1,0:T(8,128)(2,1)}, bf16[128,1024]{1,0:T(8,128)(2,1)S(1)}, u32[]{:S(2)}, u32[]{:S(2)}) %collective-permute-start.16) | collective-permute-done | bytes 262176 | tf_op jit(solution)/shard_map/ppermute | solution.py:29
  218.8 2.6 collective-permute-done.9.refs_6_
  222.5 7.1 %shard_map.67 = bf16[8,8,64,128]{3,2,1,0:T(8,128)(2,1)} custom-call(s32[2]{0:T(128)} %pad_add_fusion.zs, bf16[4,8,128,128]{3,2,1,0:T(8,128)(2,1)} %copy-done.9, bf16[4,8,128,128]{3,2,1,0:T(8,128)(2,1)} %copy-done.9, bf16[8,128,512]{2,1,0:T(8,128)(2,1)} %bitcast.29, bf16[8,128,512]{2,1,0:T(8,128)(2,1)} %bitcast.30, bf16[128,1536]{1,0:T(8,128)(2,1)} %copy-done.12, ...), custom_call_target="tpu_custom_call" | custom-call | bytes 2520000 | tf_op jit(solution)/shard_map/pallas_call | solution.py:353
  229.5 20.2 %all_to_all.20.refs_0_.refs_1_.refs_2_.refs_3_ = bf16[8,8,64,128]{3,2,1,0:T(8,128)(2,1)S(1)} all-to-all(bf16[8,8,64,128]{3,2,1,0:T(8,128)(2,1)} %shard_map.67), channel_id=1, replica_groups=mesh['q'=2,'yp'=2,'core'=2,'z'=8,'x'=4] {'core','x'}, dimensions={0} | all-to-all | bytes 2097152 | tf_op jit(solution)/shard_map/all_to_all | solution.py:459
  249.7 1.8 shard_map.68
  (112 shorter events, 23.9 us)
Async XLA Ops:
  6.5 1.3 copy-start
  11.3 25.7 %all-to-all-start.1 = ((bf16[32,24,256]{2,1,0:T(8,128)(2,1)}), bf16[32,24,256]{2,1,0:T(8,128)(2,1)S(1)}, u32[]{:S(2)}, u32[]{:S(2)}) async-start(bf16[32,24,256]{2,1,0:T(8,128)(2,1)} %bitcast.31), calls=%async_computation.1 | async-start | bytes 786432 | tf_op jit(solution)/shard_map/all_to_all | solution.py:412
  37.0 109.8 %copy-start.4 = (bf16[4,2,256,256]{3,2,1,0:T(8,128)(2,1)S(1)}, bf16[4,2,256,256]{3,2,1,0:T(8,128)(2,1)}, u32[]{:S(2)}) copy-start(bf16[4,2,256,256]{3,2,1,0:T(8,128)(2,1)} %w1.3) | copy-start | bytes 3145732
  37.0 113.0 %all-to-all-start = ((bf16[32,256,256]{2,1,0:T(8,128)(2,1)}), bf16[32,256,256]{2,1,0:T(8,128)(2,1)}, u32[]{:S(2)}, u32[]{:S(2)}) async-start(bf16[32,256,256]{2,1,0:T(8,128)(2,1)} %bitcast.28), calls=%async_computation | async-start | bytes 8388608 | tf_op jit(solution)/shard_map/all_to_all | solution.py:427
  42.2 104.6 %all-gather.4.cloned.1.call-start = ((), (), s32[]{:S(2)}) async-start(), calls=%async_computation.4 | async-start | bytes 2027520 | tf_op jit(solution)/shard_map/all_gather | solution.py:424
  43.5 3.2 %collective-permute-start = (bf16[24,768]{1,0:T(8,128)(2,1)S(1)}, bf16[24,768]{1,0:T(8,128)(2,1)S(1)}, u32[]{:S(2)}, u32[]{:S(2)}) collective-permute-start(bf16[24,768]{1,0:T(8,128)(2,1)S(1)} %fusion), channel_id=1, source_target_pairs={{0,32},{32,0},{1,33},{33,1},{2,34},{34,2},{3,35},{35,3},{4,36},{36... | collective-permute-start | bytes 110600 | tf_op jit(solution)/shard_map/ppermute | solution.py:33
  46.7 3.3 %collective-permute-start.1 = (bf16[24,768]{1,0:T(8,128)(2,1)S(1)}, bf16[24,768]{1,0:T(8,128)(2,1)S(1)}, u32[]{:S(2)}, u32[]{:S(2)}) collective-permute-start(bf16[24,768]{1,0:T(8,128)(2,1)S(1)} %add_convert_fusion.2), channel_id=1, source_target_pairs={{0,64},{64,0},{1,65},{65,1},{2,66},{66,2},{3,67},{67,3},{4,68},{68... | collective-permute-start | bytes 110600 | tf_op jit(solution)/shard_map/ppermute | solution.py:33
  50.7 170.7 %all-gather.6.cloned.1.call-start = ((), (), s32[]{:S(2)}) async-start(), calls=%async_computation.5 | async-start | bytes 1179648 | tf_op jit(solution)/shard_map/all_gather | solution.py:442
  146.8 1.5 copy-start.1
  151.7 5.2 %collective-permute-start.2 = (bf16[128,1024]{1,0:T(8,128)(2,1)S(1)}, bf16[128,1024]{1,0:T(8,128)(2,1)S(1)}, u32[]{:S(2)}, u32[]{:S(2)}) collective-permute-start(bf16[128,1024]{1,0:T(8,128)(2,1)S(1)} %get-tuple-element.25), channel_id=1, source_target_pairs={{0,32},{32,0},{1,33},{33,1},{2,34},{34,2},{3,35},{35,3},{4,36},{36... | collective-permute-start | bytes 786440 | tf_op jit(solution)/shard_map/ppermute | solution.py:33
  155.5 1.4 copy-start.3
  157.6 4.5 %collective-permute-start.3 = (bf16[4,8,256,128]{3,2,1,0:T(8,128)(2,1)}, bf16[4,8,256,128]{3,2,1,0:T(8,128)(2,1)}, u32[]{:S(2)}, u32[]{:S(2)}) collective-permute-start(bf16[4,8,256,128]{3,2,1,0:T(8,128)(2,1)} %shard_map.60), channel_id=1, source_target_pairs={{0,32},{32,0},{1,33},{33,1},{2,34},{34,2},{3,35},{35,3},{4,36},{36... | collective-permute-start | bytes 6291464 | tf_op jit(solution)/shard_map/ppermute | solution.py:33
  158.8 9.6 %collective-permute-start.5 = (bf16[128,1024]{1,0:T(8,128)(2,1)S(1)}, bf16[128,1024]{1,0:T(8,128)(2,1)S(1)}, u32[]{:S(2)}, u32[]{:S(2)}) collective-permute-start(bf16[128,1024]{1,0:T(8,128)(2,1)S(1)} %add_convert_fusion.1.a_ref), channel_id=1, source_target_pairs={{0,64},{64,0},{1,65},{65,1},{2,66},{66,2},{3,67},{67,3},{4,68},{68... | collective-permute-start | bytes 786440 | tf_op jit(solution)/shard_map/ppermute | solution.py:33
  160.3 8.1 %copy-start.2 = (bf16[768,1280]{1,0:T(8,128)(2,1)S(1)}, bf16[768,1280]{1,0:T(8,128)(2,1)}, u32[]{:S(2)}) copy-start(bf16[768,1280]{1,0:T(8,128)(2,1)} %all-gather.4.cloned.1.call-done.s_ref.p0.p1) | copy-start | bytes 5898244
  160.3 8.1 %copy-start.5 = (bf16[2,2,256,256]{3,2,1,0:T(8,128)(2,1)S(1)}, bf16[2,2,256,256]{3,2,1,0:T(8,128)(2,1)}, u32[]{:S(2)}) copy-start(bf16[2,2,256,256]{3,2,1,0:T(8,128)(2,1)} %w2.1) | copy-start | bytes 1572868
  167.1 24.9 %collective-permute-start.4 = (bf16[4,8,128,128]{3,2,1,0:T(8,128)(2,1)}, bf16[4,8,128,128]{3,2,1,0:T(8,128)(2,1)}, u32[]{:S(2)}, u32[]{:S(2)}) collective-permute-start(bf16[4,8,128,128]{3,2,1,0:T(8,128)(2,1)} %get-tuple-element.27), channel_id=1, source_target_pairs={{0,64},{64,0},{1,65},{65,1},{2,66},{66,2},{3,67},{67,3},{4,68},{68... | collective-permute-start | bytes 3145736 | tf_op jit(solution)/shard_map/ppermute | solution.py:33
  171.8 31.5 %copy-start.6 = (bf16[128,1024]{1,0:T(8,128)(2,1)}, bf16[128,1024]{1,0:T(8,128)(2,1)S(1)}, u32[]{:S(2)}) copy-start(bf16[128,1024]{1,0:T(8,128)(2,1)S(1)} %get-tuple-element.32.refs_8_) | copy-start | bytes 786436
  171.8 13.6 %collective-permute-start.6 = (bf16[128,1536]{1,0:T(8,128)(2,1)}, bf16[128,1536]{1,0:T(8,128)(2,1)S(1)}, u32[]{:S(2)}, u32[]{:S(2)}) collective-permute-start(bf16[128,1536]{1,0:T(8,128)(2,1)} %get-tuple-element.29), channel_id=1, source_target_pairs={{0,32},{32,0},{1,33},{33,1},{2,34},{34,2},{3,35},{35,3},{4,36},{36... | collective-permute-start | bytes 1179656 | tf_op jit(solution)/shard_map/ppermute | solution.py:33
  172.2 9.1 %collective-permute-start.10 = (bf16[128,1024]{1,0:T(8,128)(2,1)S(1)}, bf16[128,1024]{1,0:T(8,128)(2,1)S(1)}, u32[]{:S(2)}, u32[]{:S(2)}) collective-permute-start(bf16[128,1024]{1,0:T(8,128)(2,1)S(1)} %get-tuple-element.32.refs_8_), channel_id=1, source_target_pairs={{0,4},{4,8},{8,12},{12,16},{16,20},{20,24},{24,28},{28,0},{1,5},{5... | collective-permute-start | bytes 786440 | tf_op jit(solution)/shard_map/ppermute | solution.py:29
  173.9 7.8 %collective-permute-start.11 = (bf16[128,1024]{1,0:T(8,128)(2,1)S(1)}, bf16[128,1024]{1,0:T(8,128)(2,1)S(1)}, u32[]{:S(2)}, u32[]{:S(2)}) collective-permute-start(bf16[128,1024]{1,0:T(8,128)(2,1)S(1)} %get-tuple-element.32.refs_8_), channel_id=1, source_target_pairs={{0,28},{4,0},{8,4},{12,8},{16,12},{20,16},{24,20},{28,24},{1,29},{... | collective-permute-start | bytes 786440 | tf_op jit(solution)/shard_map/ppermute | solution.py:29
  182.7 16.2 %collective-permute-start.12 = (bf16[128,1024]{1,0:T(8,128)(2,1)}, bf16[128,1024]{1,0:T(8,128)(2,1)}, u32[]{:S(2)}, u32[]{:S(2)}) collective-permute-start(bf16[128,1024]{1,0:T(8,128)(2,1)} %get-tuple-element.34.refs_15_), channel_id=1, source_target_pairs={{0,4},{4,8},{8,12},{12,16},{16,20},{20,24},{24,28},{28,0},{1,5},{5... | collective-permute-start | bytes 786440 | tf_op jit(solution)/shard_map/ppermute | solution.py:29
  183.8 15.1 %collective-permute-start.13 = (bf16[128,1024]{1,0:T(8,128)(2,1)}, bf16[128,1024]{1,0:T(8,128)(2,1)}, u32[]{:S(2)}, u32[]{:S(2)}) collective-permute-start(bf16[128,1024]{1,0:T(8,128)(2,1)} %get-tuple-element.33.refs_9_), channel_id=1, source_target_pairs={{0,28},{4,0},{8,4},{12,8},{16,12},{20,16},{24,20},{28,24},{1,29},{... | collective-permute-start | bytes 786440 | tf_op jit(solution)/shard_map/ppermute | solution.py:29
  185.4 36.0 %copy-start.12 = (bf16[128,1536]{1,0:T(8,128)(2,1)}, bf16[128,1536]{1,0:T(8,128)(2,1)S(1)}, u32[]{:S(2)}) copy-start(bf16[128,1536]{1,0:T(8,128)(2,1)S(1)} %broadcast_select_fusion.refs_4_) | copy-start | bytes 1179652
  185.5 16.2 %collective-permute-start.7 = (bf16[128,1536]{1,0:T(8,128)(2,1)S(1)}, bf16[128,1536]{1,0:T(8,128)(2,1)S(1)}, u32[]{:S(2)}, u32[]{:S(2)}) collective-permute-start(bf16[128,1536]{1,0:T(8,128)(2,1)S(1)} %broadcast_select_fusion.refs_4_), channel_id=1, source_target_pairs={{0,1},{1,2},{2,3},{3,0},{4,5},{5,6},{6,7},{7,4},{8,9},{9,10},{10,1... | collective-permute-start | bytes 1179656 | tf_op jit(solution)/shard_map/ppermute | solution.py:29
  187.7 14.0 %collective-permute-start.8 = (bf16[128,1536]{1,0:T(8,128)(2,1)S(1)}, bf16[128,1536]{1,0:T(8,128)(2,1)S(1)}, u32[]{:S(2)}, u32[]{:S(2)}) collective-permute-start(bf16[128,1536]{1,0:T(8,128)(2,1)S(1)} %broadcast_select_fusion.refs_4_), channel_id=1, source_target_pairs={{0,3},{1,0},{2,1},{3,2},{4,7},{5,4},{6,5},{7,6},{8,11},{9,8},{10,9... | collective-permute-start | bytes 1179656 | tf_op jit(solution)/shard_map/ppermute | solution.py:29
  194.5 26.8 %all-to-all-start.2 = ((bf16[4,8,128,128]{3,2,1,0:T(8,128)(2,1)}), bf16[4,8,128,128]{3,2,1,0:T(8,128)(2,1)S(1)}, u32[]{:S(2)}, u32[]{:S(2)}) async-start(bf16[4,8,128,128]{3,2,1,0:T(8,128)(2,1)} %add_convert_fusion), calls=%async_computation.2 | async-start | bytes 2097152 | tf_op jit(solution)/shard_map/all_to_all | solution.py:451
  198.9 11.2 %collective-permute-start.14 = (bf16[128,1024]{1,0:T(8,128)(2,1)}, bf16[128,1024]{1,0:T(8,128)(2,1)S(1)}, u32[]{:S(2)}, u32[]{:S(2)}) collective-permute-start(bf16[128,1024]{1,0:T(8,128)(2,1)} %get-tuple-element.36.refs_14_), channel_id=1, source_target_pairs={{0,4},{4,8},{8,12},{12,16},{16,20},{20,24},{24,28},{28,0},{1,5},{5... | collective-permute-start | bytes 786440 | tf_op jit(solution)/shard_map/ppermute | solution.py:29
  199.9 10.2 %collective-permute-start.15 = (bf16[128,1024]{1,0:T(8,128)(2,1)}, bf16[128,1024]{1,0:T(8,128)(2,1)S(1)}, u32[]{:S(2)}, u32[]{:S(2)}) collective-permute-start(bf16[128,1024]{1,0:T(8,128)(2,1)} %get-tuple-element.35.refs_10_), channel_id=1, source_target_pairs={{0,28},{4,0},{8,4},{12,8},{16,12},{20,16},{24,20},{28,24},{1,29},{... | collective-permute-start | bytes 786440 | tf_op jit(solution)/shard_map/ppermute | solution.py:29
  203.2 18.2 %collective-permute-start.9 = (bf16[128,1536]{1,0:T(8,128)(2,1)}, bf16[128,1536]{1,0:T(8,128)(2,1)S(1)}, u32[]{:S(2)}, u32[]{:S(2)}) collective-permute-start(bf16[128,1536]{1,0:T(8,128)(2,1)} %get-tuple-element.31.refs_7_), channel_id=1, source_target_pairs={{0,1},{1,2},{2,3},{3,0},{4,5},{5,6},{6,7},{7,4},{8,9},{9,10},{10,1... | collective-permute-start | bytes 1179656 | tf_op jit(solution)/shard_map/ppermute | solution.py:29
  211.6 7.2 %collective-permute-start.16 = (bf16[128,1024]{1,0:T(8,128)(2,1)}, bf16[128,1024]{1,0:T(8,128)(2,1)S(1)}, u32[]{:S(2)}, u32[]{:S(2)}) collective-permute-start(bf16[128,1024]{1,0:T(8,128)(2,1)} %get-tuple-element.38.refs_13_), channel_id=1, source_target_pairs={{0,4},{4,8},{8,12},{12,16},{16,20},{20,24},{24,28},{28,0},{1,5},{5... | collective-permute-start | bytes 786440 | tf_op jit(solution)/shard_map/ppermute | solution.py:29
  218.8 2.6 %copy-start.19 = (bf16[128,1024]{1,0:T(8,128)(2,1)}, bf16[128,1024]{1,0:T(8,128)(2,1)S(1)}, u32[]{:S(2)}) copy-start(bf16[128,1024]{1,0:T(8,128)(2,1)S(1)} %collective-permute-done.16.refs_12_) | copy-start | bytes 786436
  222.5 27.2 %copy-start.8 = (s32[2]{0:T(128)S(1)}, s32[2]{0:T(128)}, u32[]{:S(2)}) copy-start(s32[2]{0:T(128)} %pad_add_fusion.zs) | copy-start | bytes 28
  (10 other events, 7.5 us)
Sparse Core Ops, SparseCore 0:
  50.9 95.8 all-gather.3
  175.0 35.2 all-gather.5
